TPU v7x, 128 devices: a whole 4x4x4 slice. The times are simulated.
128 devices in a mesh: branch: 2 (over core), section: 2 (over z_hi), patch: 32 (over z_lo, y, x).
Axes of the slice: x: 4, y: 4, z: 4 (z_hi: 2, z_lo: 2; z = z_hi * 2 + z_lo), core: 2. Of those that a mesh axis runs over, the one named last changes fastest.
Arguments:
- stream: bfloat16 [3840, 2560], P('patch'), may hold values from -6 to 6
- token_frame: int32 [3840], P('patch'), may hold values from 0 to 15, never falling along the last dimension, each value on 1 to 480 neighbouring positions
- frame_levels: int32 [16], replicated, may hold values from 0 to 49
- level_table: float32 [50, 7680], replicated, may hold values from -3 to 3
- branch_mod: float32 [2, 7680], P('branch'), may hold values from -2.4 to 2.4
- layer_mod: float32 [2, 7680], P('section'), may hold values from -1.8 to 1.8
- maps: float32 [2, 3, 2560], P('section'), may hold values from -3.6 to 3.6
- stale_kv: bfloat16 [2, 2, 2, 3840, 2560], P('branch', 'section', None, 'patch'), may hold values from -204 to 204
Outputs:
- guided: bfloat16 [3840, 2560], P('patch', 'branch')
- fresh_kv: bfloat16 [2, 2, 2, 3840, 2560], P('branch', 'section', None, 'patch')
Inputs may be any that keep to these rules, and one draw needn't show every extreme that they name: token_frame never falls from one token to the next, and every frame holds between 1 and 480 tokens.
All inputs are finite; a program needn't handle non-finite values.
Results may differ from a plain program's by a relative error of at most 0.025.
Values may be sent and summed in bfloat16 or wider, within the bound.
No kernel may reach another device: no remote copies, remote signals or barrier semaphores. Data moves between devices by JAX's collectives and lax.ppermute only.
A program may use at most 256 MiB of HBM per device.

v0:
```python
import jax
import jax.numpy as jnp
from jax import lax
from jax.sharding import PartitionSpec as P

HEADS = 20
HEAD_DIM = 128
FRAMES = 16
LEVELS = 50


EPSILON = 1e-06
GUIDE = 5.0


def swapped(block, axis, stride):
    count = lax.axis_size(axis)
    route = []
    for low in range(count):
        high = low | 1 << stride
        if high != low and high < count:
            route += [(low, high), (high, low)]
    return lax.ppermute(block, axis, route)


def broadcast(array, axis, root):
    mine = lax.axis_index(axis) == root
    return lax.psum(jnp.where(mine, array, jnp.zeros_like(array)), axis)


def from_behind(array, axis, by):
    count = lax.axis_size(axis)
    pairs = [(i, i + by) for i in range(count) if 0 <= i + by < count]
    return lax.ppermute(array, axis, pairs)


def fold_keys(carry, piece, start, query, patch_low, patch_rows, score_scale):
    peak, total, accum = carry
    keys, values = piece
    rows = keys.shape[0]
    heads = query.shape[1]
    head_width = query.shape[2]
    step_rows = max(1024, -(-rows // 8))
    for begin in range(0, rows, step_rows):
        count = min(step_rows, rows - begin)
        key_part = keys[begin : begin + count].reshape(count, heads, head_width)
        value_part = values[begin : begin + count].reshape(count, heads, head_width)
        scores = (
            jnp.einsum("thd,uhd->htu", query, key_part, preferred_element_type=jnp.float32)
            * score_scale
        )
        position = start + begin + jnp.arange(count, dtype=jnp.int32)
        inside = (position >= patch_low) & (position < patch_low + patch_rows)
        scores = jnp.where(inside[None, None, :], -jnp.inf, scores)
        new_peak = jnp.maximum(peak, jnp.max(scores, axis=-1))
        factor = jnp.exp(peak - new_peak)
        powers = jnp.exp(scores - new_peak[..., None])
        total = total * factor + jnp.sum(powers, axis=-1)
        accum = accum * factor[..., None] + jnp.einsum(
            "htu,uhd->htd",
            powers.astype(jnp.bfloat16),
            value_part,
            preferred_element_type=jnp.float32,
        )
        peak = new_peak
    return (peak, total, accum)


def pair_up(values_in):
    return swapped(values_in, "branch", 0)


def spread(values_in, root):
    return broadcast(values_in, "section", root)


def guide_mix(mine, other, branch_index):
    cond_out = jnp.where(branch_index == 0, mine, other).astype(jnp.float32)
    uncond_out = jnp.where(branch_index == 0, other, mine).astype(jnp.float32)
    return (uncond_out + GUIDE * (cond_out - uncond_out)).astype(jnp.bfloat16)


def guided_half(full_out, branch_index):
    half_width = full_out.shape[1] // 2
    mine = lax.dynamic_slice_in_dim(full_out, branch_index * half_width, half_width, 1)
    needed = lax.dynamic_slice_in_dim(full_out, (1 - branch_index) * half_width, half_width, 1)
    other = pair_up(needed)
    return guide_mix(mine, other, branch_index)


def body(stream, token_frame, frame_levels, level_table, branch_mod, layer_mod, maps, stale_kv):
    rows, width = stream.shape
    heads = HEADS
    head_width = HEAD_DIM
    score_scale = HEAD_DIM ** (-0.5)
    section_index = lax.axis_index("section")
    branch_index = lax.axis_index("branch")
    section_count = lax.axis_size("section")
    patch_low = lax.axis_index("patch") * rows
    level_hot = (frame_levels[:, None] == jnp.arange(LEVELS, dtype=jnp.int32)[None, :]).astype(
        jnp.float32
    )
    frame_mod = (
        jnp.dot(
            level_hot,
            level_table,
            precision=lax.Precision.HIGHEST,
            preferred_element_type=jnp.float32,
        )
        + (layer_mod[0] + branch_mod[0])[None, :]
    )
    frame_hot = (token_frame[:, None] == jnp.arange(FRAMES, dtype=jnp.int32)[None, :]).astype(
        jnp.float32
    )
    token_mod = jnp.dot(
        frame_hot, frame_mod, precision=lax.Precision.HIGHEST, preferred_element_type=jnp.float32
    )
    shift_term = token_mod[:, :width]
    scaling = token_mod[:, width : 2 * width]
    gate_term = token_mod[:, 2 * width :]
    gains = maps[0]
    stale_keys = stale_kv[0, 0, 0]
    stale_values = stale_kv[0, 0, 1]
    gathered = (
        lax.all_gather(stale_keys, "patch", axis=0, tiled=True),
        lax.all_gather(stale_values, "patch", axis=0, tiled=True),
    )

    def active(state):
        current = state[0]
        values_in = current.astype(jnp.float32)
        normed = values_in * lax.rsqrt(
            jnp.mean(values_in * values_in, axis=1, keepdims=True) + EPSILON
        )
        hidden = normed * (1.0 + scaling) + shift_term
        query = (hidden * gains[0]).astype(jnp.bfloat16)
        fresh_keys = (hidden * gains[1]).astype(jnp.bfloat16)
        fresh_values = (hidden * gains[2]).astype(jnp.bfloat16)
        query_heads = query.reshape(rows, heads, head_width)
        key_heads = fresh_keys.reshape(rows, heads, head_width)
        value_heads = fresh_values.reshape(rows, heads, head_width)
        scores = (
            jnp.einsum("thd,uhd->htu", query_heads, key_heads, preferred_element_type=jnp.float32)
            * score_scale
        )
        peak = jnp.max(scores, axis=-1)
        powers = jnp.exp(scores - peak[..., None])
        total = jnp.sum(powers, axis=-1)
        accum = jnp.einsum(
            "htu,uhd->htd",
            powers.astype(jnp.bfloat16),
            value_heads,
            preferred_element_type=jnp.float32,
        )
        peak, total, accum = fold_keys(
            (peak, total, accum), gathered, 0, query_heads, patch_low, rows, score_scale
        )
        attended = accum / total[..., None]
        attended = jnp.transpose(attended, (1, 0, 2)).reshape(rows, width)
        result = (values_in + gate_term * attended).astype(jnp.bfloat16)
        return (result, fresh_keys, fresh_values)

    def passive(state):
        return state

    blank = jnp.zeros((rows, width), jnp.bfloat16)
    state = (stream, blank, blank)
    for round_no in range(section_count):
        state = lax.cond(section_index == round_no, active, passive, state)
        if round_no + 1 < section_count:
            moved = from_behind(state[0], "section", 1)
            state = (moved, state[1], state[2])
    final, fresh_keys, fresh_values = state
    fresh_kv = jnp.stack([fresh_keys, fresh_values])[None, None]
    last_section = section_count - 1
    guided = spread(guided_half(final, branch_index), last_section)
    return (guided, fresh_kv)


def solution(mesh):
    placed = (
        P("patch", None),
        P("patch"),
        P(),
        P(),
        P("branch", None),
        P("section", None),
        P("section", None, None),
        P("branch", "section", None, "patch", None),
    )
    return jax.shard_map(
        body,
        mesh=mesh,
        in_specs=placed,
        out_specs=(P("patch", "branch"), P("branch", "section", None, "patch", None)),
        check_vma=False,
    )
```

profile of v0, /device:TPU:0, one launch (start us, length us, event | category | flops | bytes accessed | tf_op | source)
XLA Modules:
  0.0 835.6 jit_solution(26136188950147531)
XLA Ops:
  7.2 0.0 copy-start
  7.2 0.0 all-gather.7.cloned.1.call-start
  7.2 2.5 fusion.197
  9.7 0.0 all-gather.7.cloned.1.call-update
  9.8 0.0 all-gather.5.cloned.1.call-start
  9.8 0.7 all-gather.5.cloned.1.call-update
  10.5 0.0 all-reduce.2.cloned.1.call-start
  10.6 0.8 copy.168
  11.3 0.9 add_reduce_fusion
  12.2 1.4 convolution_add_fusion
  13.6 0.0 copy-start.12
  13.6 1.7 fusion.179
  15.3 1.7 fusion.196
  17.0 215.9 %all-gather.7.cloned.1.call-done = bf16[1,1,1,3840,2560]{4,3,2,1,0:T(8,128)(2,1)} async-done(((bf16[1,1,1,120,2560]{4,3,2,1,0:T(8,128)(2,1)}), bf16[1,1,1,3840,2560]{4,3,2,1,0:T(8,128)(2,1)}) %all-gather.7.cloned.1.call-update) | async-done | bytes 19660816 | tf_op jit(solution)/shard_map/all_gather | solution.py:126
  232.9 219.7 %all-gather.5.cloned.1.call-done = bf16[1,1,1,3840,2560]{4,3,2,1,0:T(8,128)(2,1)} async-done(((bf16[1,1,1,120,2560]{4,3,2,1,0:T(8,128)(2,1)}), bf16[1,1,1,3840,2560]{4,3,2,1,0:T(8,128)(2,1)}) %all-gather.5.cloned.1.call-update) | async-done | bytes 19660816 | tf_op jit(solution)/shard_map/all_gather | solution.py:125
  452.6 161.9 %conditional.2 = (bf16[120,2560]{0,1:T(8,128)(2,1)}, bf16[120,2560]{0,1:T(8,128)(2,1)S(1)}, bf16[120,2560]{0,1:T(8,128)(2,1)S(1)}) conditional(s32[]{:T(128)} %convert_element_type.78, (bf16[120,2560]{1,0:T(8,128)(2,1)S(1)}) %tuple.117, (bf16[120,2560]{1,0:T(8,128)(2,1)S(1)}, f32[120,2560]{1,0:T(8,128)}, f32[120,2560]{1,0:T(8,128)}, ...), branch_computations={%region_0.0_spmd, %region_1.13_spmd} | conditional | flops 4977483776 | bytes 418019072 | solution.py:169
  452.6 0.1 slice_reduce_fusion
  452.7 0.7 copy-done.13
  453.4 1.5 copy.114
  454.9 1.4 copy.109
  456.3 0.4 fusion.56
  456.6 2.8 copy.111
  459.4 2.7 copy.110
  462.2 3.1 multiply_convert_fusion
  465.2 1.3 multiply_convert_fusion.1
  466.6 0.5 fusion.192
  467.1 1.1 copy-done.2
  468.2 0.2 fusion.61
  468.4 25.3 %copy.113 = bf16[3840,2560]{0,1:T(8,128)(2,1)} copy(bf16[3840,2560]{1,0:T(8,128)(2,1)} %get-tuple-element.112) | data formatting | bytes 39321600 | tf_op jit(solution)/shard_map
  493.8 12.4 %fusion.190 = (bf16[1024,2560]{0,1:T(8,128)(2,1)}, bf16[1024,2560]{0,1:T(8,128)(2,1)}, bf16[1024,2560]{0,1:T(8,128)(2,1)}) fusion(bf16[3840,2560]{0,1:T(8,128)(2,1)} %copy.113), kind=kLoop, calls=%fused_computation.245 | loop fusion | bytes 31457280 | tf_op jit(solution)/shard_map/cond/branch_1_fun/slice | solution.py:47
  506.2 24.3 %copy.112 = bf16[3840,2560]{0,1:T(8,128)(2,1)} copy(bf16[3840,2560]{1,0:T(8,128)(2,1)} %get-tuple-element.111) | data formatting | bytes 39321600 | tf_op jit(solution)/shard_map
  530.5 9.2 %fusion.191 = (bf16[1024,2560]{0,1:T(8,128)(2,1)S(1)}, bf16[1024,2560]{0,1:T(8,128)(2,1)}, bf16[1024,2560]{0,1:T(8,128)(2,1)S(1)}) fusion(bf16[3840,2560]{0,1:T(8,128)(2,1)} %copy.112), kind=kLoop, calls=%fused_computation.246 | loop fusion | bytes 31457280 | tf_op jit(solution)/shard_map/cond/branch_1_fun/slice | solution.py:46
  539.8 4.4 fusion.9
  544.2 4.3 fusion.2
  548.5 5.5 fusion
  554.0 5.5 fusion.1
  559.5 9.1 %fusion.47 = f32[120,20,128]{2,0,1:T(8,128)} fusion(bf16[1024,20,128]{0,2,1:T(8,128)(2,1)} %bitcast.339, f32[20,120,1024]{2,1,0:T(8,128)} %get-tuple-element.174, f32[20,120]{1,0:T(8,128)S(1)} %get-tuple-element.145, pred[1024]{0:T(1024)(128)(4,1)S(1)} %get-tuple-element.175), kind=kOutput, calls=%fused_computation.53 | convolution fusion | flops 638976000 | bytes 16312704 | tf_op jit(solution)/shard_map/cond/branch_1_fun/htu,uhd->htd/dot_general | solution.py:59
  568.6 5.2 fusion.3
  573.8 9.2 %fusion.50 = f32[120,20,128]{2,0,1:T(8,128)} fusion(bf16[1024,20,128]{0,2,1:T(8,128)(2,1)} %bitcast.337, f32[20,120,1024]{2,1,0:T(8,128)} %get-tuple-element.170, f32[20,120]{1,0:T(8,128)S(1)} %get-tuple-element.144, pred[1024]{0:T(1024)(128)(4,1)S(1)} %get-tuple-element.176), kind=kOutput, calls=%fused_computation.54 | convolution fusion | flops 638976000 | bytes 16312704 | tf_op jit(solution)/shard_map/cond/branch_1_fun/htu,uhd->htd/dot_general | solution.py:59
  583.0 5.0 fusion.5
  588.0 6.4 fusion.53
  594.4 2.3 fusion.7
  596.7 5.4 fusion.36
  602.2 1.8 fusion.10
  604.1 0.3 copy-done.17
  604.4 0.4 copy-done.19
  604.7 3.6 fusion.60
  608.3 2.9 copy.90
  611.2 2.9 fusion.59
  614.5 2.1 copy.115
  616.7 2.1 collective-permute-start
  618.8 12.8 %collective-permute-done = bf16[120,2560]{1,0:T(8,128)(2,1)} collective-permute-done((bf16[120,2560]{1,0:T(8,128)(2,1)}, bf16[120,2560]{1,0:T(8,128)(2,1)}, u32[]{:S(2)}, u32[]{:S(2)}) %collective-permute-start) | collective-permute-done | bytes 614432 | tf_op jit(solution)/shard_map/ppermute | solution.py:34
  631.6 3.6 conditional.3
  631.6 1.1 copy.164
  632.7 1.1 copy.162
  635.3 0.0 copy-start.1
  635.3 1.1 constant_dynamic-slice_fusion
  636.4 0.1 collective-permute-start.1
  636.5 1.6 collective-permute-done.1
  638.1 1.9 fusion.178
  639.9 0.0 all-reduce.2.cloned.1.call-update
  640.0 2.4 maximum_bitcast_fusion
  642.4 184.8 %all-reduce.2.cloned.1.call-done = bf16[120,1280]{1,0:T(8,128)(2,1)} async-done(((bf16[120,1280]{1,0:T(8,128)(2,1)}), bf16[120,1280]{1,0:T(8,128)(2,1)}) %all-reduce.2.cloned.1.call-update) | async-done | bytes 307216 | tf_op jit(solution)/shard_map/psum | solution.py:28
  827.2 1.7 copy.182
  (38 shorter events, 0.1 us)
Async XLA Ops:
  7.2 5.0 copy-start
  7.2 6.4 copy-start.20
  7.2 225.7 %all-gather.7.cloned.1.call-start = ((), (), s32[]{:S(2)}) async-start(), calls=%async_computation.2 | async-start | bytes 20275200 | tf_op jit(solution)/shard_map/all_gather | solution.py:126
  9.8 442.8 %all-gather.5.cloned.1.call-start = ((), (), s32[]{:S(2)}) async-start(), calls=%async_computation.1 | async-start | bytes 20275200 | tf_op jit(solution)/shard_map/all_gather | solution.py:125
  10.5 816.7 %all-reduce.2.cloned.1.call-start = ((), (), s32[]{:S(2)}) async-start(), calls=%async_computation | async-start | bytes 614400 | tf_op jit(solution)/shard_map/psum | solution.py:28
  13.6 439.0 %copy-start.12 = (bf16[120,2560]{1,0:T(8,128)(2,1)S(1)}, bf16[120,2560]{1,0:T(8,128)(2,1)}, u32[]{:S(2)}) copy-start(bf16[120,2560]{1,0:T(8,128)(2,1)} %param.12) | copy-start | bytes 1843204
  452.6 0.8 copy-start.13
  456.3 9.0 %copy-start.4 = (bf16[120,2560]{0,1:T(8,128)(2,1)}, bf16[120,2560]{0,1:T(8,128)(2,1)S(1)}, u32[]{:S(2)}) copy-start(bf16[120,2560]{0,1:T(8,128)(2,1)S(1)} %copy.109) | copy-start | bytes 1843204 | tf_op jit(solution)/shard_map/cond
  466.6 27.2 %copy-start.10 = (bf16[120,2560]{0,1:T(8,128)(2,1)}, bf16[120,2560]{0,1:T(8,128)(2,1)S(1)}, u32[]{:S(2)}) copy-start(bf16[120,2560]{0,1:T(8,128)(2,1)S(1)} %get-tuple-element.206) | copy-start | bytes 1843204 | tf_op jit(solution)/shard_map/cond
  467.1 1.1 copy-start.2
  530.5 9.2 %slice-start.1 = ((bf16[3840,2560]{0,1:T(8,128)(2,1)}), bf16[768,2560]{0,1:T(8,128)(2,1)S(1)}, s32[]{:S(2)}) async-start(bf16[3840,2560]{0,1:T(8,128)(2,1)} %copy.112), calls=%async_computation.4 | async-start | bytes 7864320 | tf_op jit(solution)/shard_map/cond/branch_1_fun/slice | solution.py:46
  594.4 2.3 slice-start
  594.4 7.7 slice-start.4
  596.7 5.4 slice-start.5
  602.1 1.9 copy-start.3
  602.1 1.9 copy-start.7
  602.2 1.9 copy-start.15
  602.2 2.2 copy-start.17
  602.2 2.6 copy-start.19
  608.3 5.8 copy-start.8
  608.3 5.8 copy-start.11
  616.7 15.0 %collective-permute-start = (bf16[120,2560]{1,0:T(8,128)(2,1)}, bf16[120,2560]{1,0:T(8,128)(2,1)}, u32[]{:S(2)}, u32[]{:S(2)}) collective-permute-start(bf16[120,2560]{1,0:T(8,128)(2,1)} %copy.115), channel_id=1, source_target_pairs={{0,32},{1,33},{2,34},{3,35},{4,36},{5,37},{6,38},{7,39},{8,40},{9,... | collective-permute-start | bytes 1843208 | tf_op jit(solution)/shard_map/ppermute | solution.py:34
  635.3 193.6 %copy-start.1 = (f32[50,7680]{1,0:T(8,128)S(1)}, f32[50,7680]{1,0:T(8,128)}, u32[]{:S(2)}) copy-start(f32[50,7680]{1,0:T(8,128)} %param.15) | copy-start | bytes 4608004
  636.4 1.7 collective-permute-start.1
Sparse Core Ops, SparseCore 0:
  9.9 222.9 all-gather.6
  234.6 217.9 all-gather.4
  640.1 187.0 all-reduce.1
where the time goes:
time: 845 us; the launch traced here: 836 us
  waiting for transfers between devices  636 us (75%)
  local copies, waits for them, and re-layouts  97.2 us (12%)
  matrix products  56.9 us (7%)
  other arithmetic  27.4 us (3%)
  between operations  14.1 us (2%)
    all_gather x1, waiting for transfers between devices, body(): lax.all_gather(stale_keys, 'patch', axis=0, tiled=True)  220 us
    all_gather x1, waiting for transfers between devices, body(): lax.all_gather(stale_values, 'patch', axis=0, tiled=True)  216 us
    psum x1, waiting for transfers between devices, broadcast(): return lax.psum(jnp.where(mine, array, jnp.zeros_like(array)), axis)  185 us
    another operation x6, local copies, waits for them, and re-layouts  58.1 us
    dot_general x4, matrix products, fold_keys(): jnp.einsum('htu,uhd->htd', powers.astype(jnp.bfloat16), value_part, prefe...  30 us
    dot_general x4, matrix products, fold_keys(): jnp.einsum('thd,uhd->htu', query, key_part, preferred_element_type=jnp.fl...  19.7 us
  transfers between devices with their start and end apart: 5, of which 5 were waited for; matrix products, arithmetic and copies ran while one was open for 1% of the time, Pallas kernels for 0%

commit v1 on v0

v1 whole, which is shorter than its diff:
```python
import functools
import math

import jax
import jax.numpy as jnp
from jax import lax
from jax.experimental import pallas as pl
from jax.experimental.pallas import tpu as pltpu
from jax.sharding import PartitionSpec as P

HEADS = 20
HEAD_DIM = 128
FRAMES = 16
LEVELS = 50
TOK = 120
THIRD = 40
PATCHES = 32
WIDTH = HEADS * HEAD_DIM
EPSILON = 1e-06
GUIDE = 5.0
BIG = 1e30
PLANE = ("section", "patch")
F32 = jnp.float32
BF16 = jnp.bfloat16
VMEM_BYTES = 56 * 1024 * 1024
PARAMS = pltpu.CompilerParams(vmem_limit_bytes=VMEM_BYTES)

OWN_ROWS = PATCHES * THIRD
TILE = 4 * THIRD
CHUNK = 320
MID = 64


def place_of(head, third):
    if head < 16:
        return 4 * head + third
    return 16 * (head - 16) + 4 * third + 3


def dot(a, b, dims):
    return lax.dot_general(a, b, (dims, ((), ())), preferred_element_type=F32)


NN = ((1,), (0,))
NT = ((1,), (1,))
TN = ((0,), (0,))


def split3(v):
    hi = v.astype(BF16).astype(F32)
    mid = (v - hi).astype(BF16).astype(F32)
    low = (v - hi - mid).astype(BF16).astype(F32)
    return hi, mid, low


def turned(rows, third):
    cut = THIRD * third
    return rows if cut == 0 else jnp.concatenate([rows[cut:TOK], rows[:cut]], axis=0)


def pack_kernel(scal, kv, kv_more, x, x_more, stream, frames, out, aux):
    step = pl.program_id(0)
    section = scal[0]

    @pl.when(step == 0)
    def _():
        values = stream[...].astype(F32)
        square = values * values
        ones = jnp.ones((8, WIDTH), BF16)
        row = lax.broadcasted_iota(jnp.int32, (8, 128), 0)
        lane = lax.broadcasted_iota(jnp.int32, (8, 128), 1)
        for third in range(3):
            t = jnp.concatenate([turned(square, third), jnp.zeros((8, WIDTH), F32)], axis=0)
            hi = t.astype(BF16)
            low = (t - hi.astype(F32)).astype(BF16)
            total = dot(ones, hi, NT) + dot(ones, low, NT)
            r = jnp.where(lane < TOK, lax.rsqrt(total * (1.0 / WIDTH) + EPSILON), 0.0)
            hi, mid, low = split3(r)
            a = jnp.where(row == 0, hi, jnp.where(row == 1, mid, jnp.where(row == 2, low, 0.0)))
            aux[third] = jnp.where(row == 3, frames[third : third + 1, :], a)

    def halves(block):
        values = block[...].astype(F32)
        parts = []
        for third in range(3):
            t = turned(values, third)
            parts.append(jnp.where(section == 0, t[0:64], t[TOK - 64 : TOK]))
        return parts

    none = jnp.zeros((8, 128), F32)
    keys = kv[0].astype(F32)
    vals = jnp.concatenate([kv[1].astype(F32), none], axis=0).astype(BF16)
    xs = halves(x)
    for third in range(3):
        out[third, 0:128] = jnp.concatenate([keys, aux[third]], axis=0).astype(BF16)
        out[third, 128:256] = vals
        out[third, 256:CHUNK] = xs[third].astype(BF16)
    y = lax.rem(step, 4)
    keys = kv_more[0].astype(F32)
    vals = jnp.concatenate([kv_more[1].astype(F32), none], axis=0).astype(BF16)
    xs = halves(x_more)
    which = jnp.where(y == 3, 0, y)
    out[3, 0:128] = jnp.concatenate([keys, aux[which]], axis=0).astype(BF16)
    out[3, 128:256] = vals
    chosen = jnp.where(which == 0, xs[0], jnp.where(which == 1, xs[1], xs[2]))
    out[3, 256:CHUNK] = chosen.astype(BF16)


def pack(section, stale, stream, frames):
    grid = pltpu.PrefetchScalarGridSpec(
        num_scalar_prefetch=1,
        grid=(16,),
        in_specs=[
            pl.BlockSpec((2, TOK, 128), lambda r, s: (0, 0, r)),
            pl.BlockSpec((2, TOK, 128), lambda r, s: (0, 0, 16 + r // 4)),
            pl.BlockSpec((TOK, 128), lambda r, s: (0, r)),
            pl.BlockSpec((TOK, 128), lambda r, s: (0, 16 + r // 4)),
            pl.BlockSpec((TOK, WIDTH), lambda r, s: (0, 0)),
            pl.BlockSpec((8, 128), lambda r, s: (0, 0)),
        ],
        out_specs=pl.BlockSpec((4, CHUNK, 128), lambda r, s: (r, 0, 0)),
        scratch_shapes=[pltpu.VMEM((3, 8, 128), F32)],
    )
    return pl.pallas_call(
        pack_kernel,
        grid_spec=grid,
        out_shape=jax.ShapeDtypeStruct((64, CHUNK, 128), BF16),
        compiler_params=PARAMS,
        name="pack",
    )(section, stale, stale, stream, stream, stream, frames)


def mod_table(frame_mod, with_scale):
    hi, mid, low = split3(frame_mod)
    table = jnp.concatenate([hi, mid, low, jnp.zeros((16, frame_mod.shape[1]), F32)], axis=0)
    if with_scale:
        row = lax.broadcasted_iota(jnp.int32, (64, 128), 0)
        extra = jnp.where((row >= 48) & (row < 51), 1.0, 0.0)
        table = jnp.concatenate([table, extra], axis=1)
    return table.astype(BF16)


def hot_rows(aux):
    row = lax.broadcasted_iota(jnp.int32, (48, 128), 0)
    hot = jnp.where((row & 15).astype(F32) == aux[3:4, :], 1.0, 0.0)
    return jnp.concatenate([hot, aux, jnp.zeros((8, 128), F32)], axis=0).astype(BF16)


def place_keys(p, kv, ka, va):
    row = lax.broadcasted_iota(jnp.int32, (128, 128), 0)
    col = lax.broadcasted_iota(jnp.int32, (128, 128), 1)
    at = pl.ds(pl.multiple_of(p * 128, 128), 128)
    hidden = (col == p) | ((col == PATCHES) & (row >= TOK))
    ka[at, 0:128] = kv[0, p, 0:128, :]
    ka[at, 128:256] = jnp.where(hidden, -BIG, 0.0).astype(BF16)
    va[at, 0:128] = kv[0, p, 128:256, :]
    va[at, 128:256] = jnp.ones((128, 128), BF16)


def place_fresh(p, hid, maps, fk, fv):
    row = lax.broadcasted_iota(jnp.int32, (128, 128), 0)
    col = lax.broadcasted_iota(jnp.int32, (128, 128), 1)
    at = pl.ds(pl.multiple_of(p * 128, 128), 128)
    fk[at, 0:128] = (hid * maps[1:2, :]).astype(BF16)
    fk[at, 128:256] = jnp.where((col == PATCHES) & (row >= TOK), -BIG, 0.0).astype(BF16)
    fv[at, 0:128] = (hid * maps[2:3, :]).astype(BF16)
    fv[at, 128:256] = jnp.ones((128, 128), BF16)


def place_query(t, pair_hid, maps, qa):
    row = lax.broadcasted_iota(jnp.int32, (80, 128), 0)
    col = lax.broadcasted_iota(jnp.int32, (80, 128), 1)
    patch = 2 * t + jnp.where(row >= THIRD, 1, 0)
    at = pl.ds(pl.multiple_of(t * 80, 16), 80)
    qa[at, 0:128] = (pair_hid * maps[0:1, :]).astype(BF16)
    qa[at, 128:256] = jnp.where((col == patch) | (col == PATCHES), 1.0, 0.0).astype(BF16)


def attention(qa, ka, va, fk, fv, xo, go, sc, pc, result):
    factor = HEAD_DIM ** (-0.5) * math.log2(math.e)
    keys = ka.shape[0]
    step = 512

    @pl.loop(0, OWN_ROWS // TILE)
    def _(tile):
        at = pl.ds(pl.multiple_of(tile * TILE, 16), TILE)
        q = qa[at, :]
        top = None
        for begin in range(0, keys, step):
            s = dot(q, ka[begin : begin + step, :], NT)
            sc[:, begin : begin + step] = s
            for lane in range(0, step, 128):
                part = s[:, lane : lane + 128]
                top = part if top is None else jnp.maximum(top, part)
        fresh = []
        for pair in range(2):
            low = pl.multiple_of(tile * TILE + pair * 80, 16)
            klow = pl.multiple_of((tile * 4 + pair * 2) * 128, 256)
            s = dot(qa[pl.ds(low, 80), :], fk[pl.ds(klow, 256), :], NT)
            fresh.append(s[0:THIRD, 0:128])
            fresh.append(s[THIRD:80, 128:256])
        fresh = jnp.concatenate(fresh, axis=0)
        top = jnp.max(jnp.maximum(top, fresh), axis=1, keepdims=True)
        for begin in range(0, keys, step):
            pc[:, begin : begin + step] = jnp.exp2((sc[:, begin : begin + step] - top) * factor).astype(BF16)
        total = dot(pc[...], va[...], NN)
        power = jnp.exp2((fresh - top) * factor)
        none = jnp.zeros((THIRD, 128), F32)
        added = []
        for pair in range(2):
            a = power[pair * 80 : pair * 80 + THIRD]
            b = power[pair * 80 + THIRD : pair * 80 + 80]
            both = jnp.concatenate(
                [jnp.concatenate([a, none], axis=1), jnp.concatenate([none, b], axis=1)], axis=0
            ).astype(BF16)
            klow = pl.multiple_of((tile * 4 + pair * 2) * 128, 256)
            added.append(dot(both, fv[pl.ds(klow, 256), :], NN))
        total = total + jnp.concatenate(added, axis=0)
        attended = total[:, 0:128] / total[:, 128:256]
        result(at, (xo[at, :] + go[at, :] * attended).astype(BF16))


def first_kernel(kv, x_rest, frame_mod, maps, x_out, mid, qa, ka, va, fk, fv, xo, go, sc, pc, sq):
    table = mod_table(frame_mod[...], True)
    gains = maps[...]

    @pl.loop(0, 4)
    def _(block):
        for sub in range(4):
            t = block * 4 + sub
            hids, xs, gates = [], [], []
            for half in range(2):
                p = 2 * t + half
                aux = kv[0, p, 112:128, :].astype(F32)[8:16]
                xa = kv[0, p, 256:CHUNK, :].astype(F32)
                xb = x_rest[0, p].astype(F32)[8:64]
                x = jnp.concatenate([xa, xb, jnp.zeros((8, 128), F32)], axis=0)
                m = dot(hot_rows(aux), table, TN)
                hid = x * m[:, 384:512] * (1.0 + m[:, 128:256]) + m[:, 0:128]
                place_keys(p, kv, ka, va)
                place_fresh(p, hid, gains, fk, fv)
                hids.append(hid[0:THIRD])
                xs.append(x[0:THIRD])
                gates.append(m[0:THIRD, 256:384])
            place_query(t, jnp.concatenate(hids, axis=0), gains, qa)
            at = pl.ds(pl.multiple_of(t * 80, 16), 80)
            xo[at, :] = jnp.concatenate(xs, axis=0)
            go[at, :] = jnp.concatenate(gates, axis=0)

    def result(at, value):
        x_out[at, :] = value
        wide = value.astype(F32)
        sq[at, :] = wide * wide

    attention(qa, ka, va, fk, fv, xo, go, sc, pc, result)
    square = sq[...]
    hi = square.astype(BF16)
    low = (square - hi.astype(F32)).astype(BF16)
    ones = jnp.ones((8, 128), BF16)
    total = dot(ones, hi, NT) + dot(ones, low, NT)
    hi = total.astype(BF16).astype(F32)
    low = total - hi
    rows = [part[0:1, 128 * i : 128 * i + 128] for part in (hi, low) for i in range(10)]
    sums = jnp.concatenate(rows + [jnp.zeros((4, 128), F32)], axis=0)
    for t in range(PATCHES // 2):
        pair = x_out[80 * t : 80 * t + 80, :].astype(F32)
        for half in range(2):
            p = 2 * t + half
            block = jnp.concatenate([pair[THIRD * half : THIRD * half + THIRD], sums], axis=0).astype(BF16)
            mid[p] = block
            mid[PATCHES + p] = block


SCRATCH = [
    pltpu.VMEM((OWN_ROWS, 256), BF16),
    pltpu.VMEM((PATCHES * 128, 256), BF16),
    pltpu.VMEM((PATCHES * 128, 256), BF16),
    pltpu.VMEM((PATCHES * 128, 256), BF16),
    pltpu.VMEM((PATCHES * 128, 256), BF16),
    pltpu.VMEM((OWN_ROWS, 128), F32),
    pltpu.VMEM((OWN_ROWS, 128), F32),
    pltpu.VMEM((TILE, PATCHES * 128), F32),
    pltpu.VMEM((TILE, PATCHES * 128), BF16),
]


def first_layer(received, frame_mod, maps):
    return pl.pallas_call(
        first_kernel,
        grid=(1,),
        in_specs=[
            pl.BlockSpec((1, PATCHES, CHUNK, 128), lambda i: (0, 0, 0, 0)),
            pl.BlockSpec((1, PATCHES, 64, 128), lambda i: (1, 0, 4, 0)),
            pl.BlockSpec((16, 384), lambda i: (0, 0)),
            pl.BlockSpec((3, 128), lambda i: (0, 0)),
        ],
        out_specs=[
            pl.BlockSpec((OWN_ROWS, 128), lambda i: (0, 0)),
            pl.BlockSpec((64, MID, 128), lambda i: (0, 0, 0)),
        ],
        out_shape=[
            jax.ShapeDtypeStruct((OWN_ROWS, 128), BF16),
            jax.ShapeDtypeStruct((64, MID, 128), BF16),
        ],
        scratch_shapes=SCRATCH + [pltpu.VMEM((OWN_ROWS, 128), F32)],
        compiler_params=PARAMS,
        name="first_layer",
    )(received, received, frame_mod, maps)


def second_kernel(scal, kv, own, after, before, sums, frame_mod, maps, x_out, qa, ka, va, fk, fv, xo, go, sc, pc, rs):
    table = mod_table(frame_mod[...], False)
    gains = maps[...]
    third = scal[0]
    row = lax.broadcasted_iota(jnp.int32, (16, OWN_ROWS), 0)
    ones = jnp.where(lax.broadcasted_iota(jnp.int32, (16, 128), 0) < 3, 1.0, 0.0).astype(BF16)
    for k in range(3):
        which = lax.rem(third + k, 3)
        total = None
        for head in range(HEADS):
            at = 4 * head + which if head < 16 else 16 * (head - 16) + 4 * which + 3
            part = sums[at].astype(F32)
            total = part if total is None else total + part
        square = jnp.concatenate([total[8 + i : 9 + i] + total[18 + i : 19 + i] for i in range(10)], axis=1)
        hi, mid, low = split3(lax.rsqrt(square * (1.0 / WIDTH) + EPSILON))
        r = jnp.where(row == 0, hi, jnp.where(row == 1, mid, jnp.where(row == 2, low, 0.0)))
        rs[k] = dot(r.astype(BF16), ones, TN)

    @pl.loop(0, 4)
    def _(block):
        for sub in range(4):
            t = block * 4 + sub
            at = pl.ds(pl.multiple_of(t * 80, 16), 80)
            pair = [ref[at, :].astype(F32) for ref in (own, after, before)]
            scale = [rs[k, at, :] for k in range(3)]
            hids, gates = [], []
            for half in range(2):
                p = 2 * t + half
                cut = slice(THIRD * half, THIRD * half + THIRD)
                aux = kv[0, p, 112:128, :].astype(F32)[8:16]
                none = [jnp.zeros((8, 128), F32)]
                x = jnp.concatenate([v[cut] for v in pair] + none, axis=0)
                r = jnp.concatenate([v[cut] for v in scale] + none, axis=0)
                m = dot(hot_rows(aux), table, TN)
                hid = x * r * (1.0 + m[:, 128:256]) + m[:, 0:128]
                place_keys(p, kv, ka, va)
                place_fresh(p, hid, gains, fk, fv)
                hids.append(hid[0:THIRD])
                gates.append(m[0:THIRD, 256:384])
            place_query(t, jnp.concatenate(hids, axis=0), gains, qa)
            xo[at, :] = pair[0]
            go[at, :] = jnp.concatenate(gates, axis=0)

    def result(at, value):
        x_out[at, :] = value

    attention(qa, ka, va, fk, fv, xo, go, sc, pc, result)


def second_layer(third, received, own, after, before, sums, frame_mod, maps):
    rows = pl.BlockSpec((OWN_ROWS, 128), lambda i, s: (0, 0))
    grid = pltpu.PrefetchScalarGridSpec(
        num_scalar_prefetch=1,
        grid=(1,),
        in_specs=[
            pl.BlockSpec((1, PATCHES, 256, 128), lambda i, s: (1, 0, 0, 0)),
            rows,
            rows,
            rows,
            pl.BlockSpec((64, 32, 128), lambda i, s: (0, 1, 0)),
            pl.BlockSpec((16, 384), lambda i, s: (0, 0)),
            pl.BlockSpec((3, 128), lambda i, s: (0, 0)),
        ],
        out_specs=rows,
        scratch_shapes=SCRATCH + [pltpu.VMEM((3, OWN_ROWS, 128), F32)],
    )
    return pl.pallas_call(
        second_kernel,
        grid_spec=grid,
        out_shape=jax.ShapeDtypeStruct((OWN_ROWS, 128), BF16),
        compiler_params=PARAMS,
        name="second_layer",
    )(third, received, own, after, before, sums, frame_mod, maps)


def home_kernel(scal, got, stream, frames, frame_mod, maps, out, xs):
    section = scal[0]
    square = jnp.zeros((TOK, 128), F32)
    for head in range(HEADS):
        cols = slice(128 * head, 128 * head + 128)
        parts = [got[place_of(head, third)].astype(F32)[0:THIRD] for third in range(3)]
        x = jnp.where(section == 0, stream[:, cols].astype(F32), jnp.concatenate(parts, axis=0))
        xs[:, cols] = x
        square = square + x * x
    r = lax.rsqrt(jnp.sum(square, axis=1, keepdims=True) * (1.0 / WIDTH) + EPSILON)
    row = lax.broadcasted_iota(jnp.int32, (48, 128), 0)
    hot = jnp.where((row & 15).astype(F32) == frames[0:1, :], 1.0, 0.0).astype(BF16)
    for head in range(HEADS):
        cols = slice(128 * head, 128 * head + 128)
        more = slice(WIDTH + 128 * head, WIDTH + 128 * head + 128)
        mod = jnp.concatenate([frame_mod[:, cols], frame_mod[:, more]], axis=1)
        m = dot(hot, jnp.concatenate(split3(mod), axis=0).astype(BF16), TN)[0:TOK]
        hid = xs[:, cols] * r * (1.0 + m[:, 128:256]) + m[:, 0:128]
        out[0, :, cols] = (hid * maps[1:2, cols]).astype(BF16)
        out[1, :, cols] = (hid * maps[2:3, cols]).astype(BF16)


def home(section, got, stream, frames, frame_mod, maps):
    whole = pl.BlockSpec(memory_space=pltpu.VMEM)
    return pl.pallas_call(
        home_kernel,
        in_specs=[pl.BlockSpec(memory_space=pltpu.SMEM)] + [whole] * 5,
        out_specs=whole,
        out_shape=jax.ShapeDtypeStruct((2, TOK, WIDTH), BF16),
        scratch_shapes=[pltpu.VMEM((TOK, WIDTH), F32)],
        compiler_params=PARAMS,
        name="home",
    )(section, got, stream, frames, frame_mod, maps)


def unpack_kernel(scal, got, out):
    branch = scal[0]
    for j in range(HEADS // 2):
        parts = []
        for third in range(3):
            a, b = place_of(j, third), place_of(j + HEADS // 2, third)
            parts.append(got[jnp.where(branch == 0, a, b)].astype(F32))
        out[:, 128 * j : 128 * j + 128] = jnp.concatenate(parts, axis=0).astype(BF16)


def unpack(branch, got):
    whole = pl.BlockSpec(memory_space=pltpu.VMEM)
    return pl.pallas_call(
        unpack_kernel,
        in_specs=[pl.BlockSpec(memory_space=pltpu.SMEM), whole],
        out_specs=whole,
        out_shape=jax.ShapeDtypeStruct((TOK, WIDTH // 2), BF16),
        compiler_params=PARAMS,
        name="unpack",
    )(branch, got)


def body(stream, token_frame, frame_levels, level_table, branch_mod, layer_mod, maps, stale_kv):
    section = lax.axis_index("section")
    branch = lax.axis_index("branch")
    place = section * PATCHES + lax.axis_index("patch")
    x, y, z = place % 4, (place // 4) % 4, place // 16
    head = jnp.where(x < 3, place // 4, 16 + z)
    third = jnp.where(x < 3, x, jnp.where(y < 3, y, 0))

    both = jnp.concatenate([layer_mod.reshape(3, WIDTH), maps[0]], axis=0)
    other = lax.ppermute(both, "section", [(0, 1), (1, 0)])

    tf = token_frame.astype(F32)
    frames = jnp.stack([jnp.pad(jnp.roll(tf, -THIRD * k), (0, 8), constant_values=-1.0) for k in range(3)])
    frames = jnp.pad(frames, ((0, 5), (0, 0)))
    section_at = section.reshape(1).astype(jnp.int32)
    send = pack(section_at, stale_kv[0, 0], stream, frames)
    received = lax.all_to_all(send, PLANE, 0, 0, tiled=True)
    received = received.reshape(2, PATCHES, CHUNK, 128)

    level_hot = (frame_levels[:, None] == jnp.arange(LEVELS, dtype=jnp.int32)[None, :]).astype(F32)
    base = jnp.dot(level_hot, level_table, precision=lax.Precision.HIGHEST, preferred_element_type=F32)
    home_mod = base + (layer_mod[0] + branch_mod[0])[None, :]

    def of_head(array):
        rows = array.shape[0]
        return lax.dynamic_slice_in_dim(array.reshape(rows, -1, HEADS, 128), head, 1, 2)[:, :, 0]

    layers = jnp.stack([jnp.where(section == 0, both, other), jnp.where(section == 0, other, both)])
    mine = of_head(layers.reshape(12, WIDTH)).reshape(2, 6, 128)
    base_mine = of_head(base)
    branch_mine = of_head(branch_mod)[0]
    mods = base_mine[None] + (mine[:, 0:3] + branch_mine[None])[:, None]
    mods = mods.reshape(2, FRAMES, 384)
    gains = mine[:, 3:6]

    x_one, mid = first_layer(received, mods[0], gains[0])

    def from_third(by):
        pairs = [(place_of(h, (g + by) % 3), place_of(h, g)) for h in range(HEADS) for g in range(3)]
        return lax.ppermute(x_one, PLANE, pairs)

    after, before = from_third(1), from_third(2)
    mid_got = lax.all_to_all(mid, PLANE, 0, 0, tiled=True)
    fresh = home(section_at, mid_got, stream, frames, home_mod, maps[0])
    x_two = second_layer(third.reshape(1).astype(jnp.int32), received, x_one, after, before, mid_got, mods[1], gains[1])

    x_other = lax.ppermute(x_two, "branch", [(0, 1), (1, 0)])
    cond = jnp.where(branch == 0, x_two, x_other).astype(F32)
    uncond = jnp.where(branch == 0, x_other, x_two).astype(F32)
    guided = (uncond + GUIDE * (cond - uncond)).astype(BF16).reshape(1, PATCHES, THIRD, 128)
    guided = jnp.broadcast_to(guided, (2, PATCHES, THIRD, 128)).reshape(64, THIRD, 128)
    guided_got = lax.all_to_all(guided, PLANE, 0, 0, tiled=True)
    out = unpack(branch.reshape(1).astype(jnp.int32), guided_got)
    return (out, fresh[None, None])


def solution(mesh):
    placed = (
        P("patch", None),
        P("patch"),
        P(),
        P(),
        P("branch", None),
        P("section", None),
        P("section", None, None),
        P("branch", "section", None, "patch", None),
    )
    return jax.shard_map(
        body,
        mesh=mesh,
        in_specs=placed,
        out_specs=(P("patch", "branch"), P("branch", "section", None, "patch", None)),
        check_vma=False,
    )
```

time: 845 us -> 207 us (0.24)
  waiting for transfers between devices: 636 us -> 90.6 us
  local copies, waits for them, and re-layouts: 97.2 us -> 5.01 us
  Pallas kernels: 0 us -> 60.5 us
  matrix products: 56.9 us -> 1.49 us
  starting transfers between devices: 2.34 us -> 44.7 us
  other arithmetic: 27.4 us -> 2.94 us
  between operations: 14.1 us -> 0.92 us
    all_gather x2 -> x0, waiting for transfers between devices: 436 us -> none  [the longest x1 220 us: body(): lax.all_gather(stale_keys, 'patch', axis=0, tiled=True)]
    psum x1 -> x0, waiting for transfers between devices: 185 us -> none  [broadcast(): return lax.psum(jnp.where(mine, array, jnp.zeros_like(array)), axis)]
    pallas_call x0 -> x5, Pallas kernels: none -> 60.5 us  [the longest x1 22.1 us: first_layer(): pl.pallas_call(first_kernel, grid=(1,), in_specs=[pl.BlockSpec((1, PATCHE...]
    all_to_all x0 -> x3, waiting for transfers between devices: none -> 58.7 us  [the longest x1 46.9 us: body(): received = lax.all_to_all(send, PLANE, 0, 0, tiled=True)]
    another operation x6 -> x3, local copies, waits for them, and re-layouts: 58.1 us -> 0.04 us  [the longest x1 0.03 us: of_head(): array.reshape(rows, -1, HEADS, 128)]
    dot_general x11 -> x0, matrix products: 55.5 us -> none  [the longest x4 30 us: fold_keys(): jnp.einsum('htu,uhd->htd', powers.astype(jnp.bfloat16), value_part, prefe...]
    all_to_all x0 -> x3, starting transfers between devices: none -> 34.6 us  [the longest x1 11.9 us: body(): received = lax.all_to_all(send, PLANE, 0, 0, tiled=True)]
    slice x9 -> x3, local copies, waits for them, and re-layouts: 26 us -> 0.16 us  [the longest x2 0.15 us: body(): jnp.roll(tf, -THIRD * k)]
  transfers between devices with their start and end apart: 5 -> 7, of which waited for: 5 -> 6; matrix products, arithmetic and copies ran while one was open for 1% -> 2% of each run, Pallas kernels for 0% -> 2%
where the time goes in v1:
time: 207 us; the launch traced here: 206 us
  waiting for transfers between devices  90.6 us (44%)
  Pallas kernels  60.5 us (29%)
  starting transfers between devices  44.7 us (22%)
  local copies, waits for them, and re-layouts  5.01 us (2%)
  other arithmetic  2.94 us (1%)
    all_to_all x1, waiting for transfers between devices, body(): received = lax.all_to_all(send, PLANE, 0, 0, tiled=True)  46.9 us
    pallas_call x1, Pallas kernels, first_layer(): pl.pallas_call(first_kernel, grid=(1,), in_specs=[pl.BlockSpec((1, PATCHE...  22.1 us
    pallas_call x1, Pallas kernels, second_layer(): pl.pallas_call(second_kernel, grid_spec=grid, out_shape=jax.ShapeDtypeStr...  21.9 us
    ppermute x2, waiting for transfers between devices, from_third(): return lax.ppermute(x_one, PLANE, pairs)  17.2 us
    ppermute x1, waiting for transfers between devices, body(): other = lax.ppermute(both, 'section', [(0, 1), (1, 0)])  12.8 us
    all_to_all x1, starting transfers between devices, body(): received = lax.all_to_all(send, PLANE, 0, 0, tiled=True)  11.9 us
    all_to_all x1, waiting for transfers between devices, body(): guided_got = lax.all_to_all(guided, PLANE, 0, 0, tiled=True)  11.8 us
    all_to_all x1, starting transfers between devices, body(): mid_got = lax.all_to_all(mid, PLANE, 0, 0, tiled=True)  11.4 us
  transfers between devices with their start and end apart: 7, of which 6 were waited for; matrix products, arithmetic and copies ran while one was open for 2% of the time, Pallas kernels for 2%

profile of v1, /device:TPU:0, one launch (start us, length us, event | category | flops | bytes accessed | tf_op | source)
XLA Modules:
  0.0 206.0 jit_solution(16371342757245225360)
XLA Ops:
  0.6 0.0 copy-start
  0.6 0.8 convert_element_type.15
  1.4 0.1 fusion.7
  1.5 0.1 fusion.8
  1.6 0.1 fusion.4
  1.7 0.6 select_maximum_fusion.frames
  2.3 11.3 %pack.1 = bf16[64,320,128]{2,1,0:T(8,128)(2,1)} custom-call(s32[1]{0:T(128)} %bitcast.2.scal, bf16[2,120,2560]{2,1,0:T(8,128)(2,1)} %bitcast.42, bf16[2,120,2560]{2,1,0:T(8,128)(2,1)} %bitcast.43, bf16[120,2560]{1,0:T(8,128)(2,1)} %stream.3, bf16[120,2560]{1,0:T(8,128)(2,1)} %stream.3, bf16[120,2560]{1,0:T(8,128)(2,1)} %stream.3, ...), custom_call_target="tpu_custom_call" | custom-call | tf_op jit(solution)/shard_map/pack/pallas_call | solution.py:124
  13.5 0.0 copy-start.8
  13.5 0.0 copy-start.6
  13.5 0.0 copy-start.7
  13.5 0.0 copy-start.9
  13.6 11.9 %all-to-all-start = ((bf16[64,320,128]{2,1,0:T(8,128)(2,1)}), bf16[64,320,128]{2,1,0:T(8,128)(2,1)}, u32[]{:S(2)}, u32[]{:S(2)}) async-start(bf16[64,320,128]{2,1,0:T(8,128)(2,1)} %pack.1), calls=%async_computation | async-start | bytes 10485760 | tf_op jit(solution)/shard_map/all_to_all | solution.py:459
  25.4 0.0 copy-done.8
  25.5 0.0 copy-done.6
  25.5 0.0 copy-done.7
  25.5 0.0 copy-start.3
  25.5 0.2 add_reduce_fusion
  25.8 3.2 %collective-permute-start = (f32[6,2560]{1,0:T(8,128)S(1)}, f32[6,2560]{1,0:T(8,128)S(1)}, u32[]{:S(2)}, u32[]{:S(2)}) collective-permute-start(f32[6,2560]{1,0:T(8,128)S(1)} %pad_maximum_fusion.1), channel_id=1, source_target_pairs={{0,32},{32,0},{1,33},{33,1},{2,34},{34,2},{3,35},{35,3},{4,36},{36... | collective-permute-start | bytes 184328 | tf_op jit(solution)/shard_map/ppermute | solution.py:452
  29.0 0.0 copy-done
  29.0 0.0 copy-done.9
  29.0 1.5 broadcast_add_fusion
  30.5 0.1 reshape.43
  30.7 12.8 %collective-permute-done = f32[6,2560]{1,0:T(8,128)S(1)} collective-permute-done((f32[6,2560]{1,0:T(8,128)S(1)}, f32[6,2560]{1,0:T(8,128)S(1)}, u32[]{:S(2)}, u32[]{:S(2)}) %collective-permute-start) | collective-permute-done | bytes 61472 | tf_op jit(solution)/shard_map/ppermute | solution.py:452
  43.4 0.0 copy-done.3
  43.6 0.6 copy.24
  44.2 0.6 slice_bitcast_fusion
  44.8 46.9 %all-to-all-done = bf16[64,320,128]{2,1,0:T(8,128)(2,1)} async-done(((bf16[64,320,128]{2,1,0:T(8,128)(2,1)}), bf16[64,320,128]{2,1,0:T(8,128)(2,1)}, u32[]{:S(2)}, u32[]{:S(2)}) %all-to-all-start) | async-done | bytes 5242912 | tf_op jit(solution)/shard_map/all_to_all | solution.py:459
  91.8 22.1 %first_layer.1 = (bf16[1280,128]{1,0:T(8,128)(2,1)}, bf16[64,64,128]{2,1,0:T(8,128)(2,1)}) custom-call(bf16[2,32,320,128]{3,2,1,0:T(8,128)(2,1)} %bitcast.7.kv.x_rest, bf16[2,32,320,128]{3,2,1,0:T(8,128)(2,1)} %bitcast.7.kv.x_rest, f32[16,384]{1,0:T(8,128)} %bitcast.52, f32[3,128]{1,0:T(4,128)} %get-tuple-element.14.maps), custom_call_target="tpu_custom_call" | custom-call | tf_op jit(solution)/shard_map/first_layer/pallas_call | solution.py:288
  113.9 0.0 copy-start.4
  113.9 11.4 %all-to-all-start.1 = ((bf16[64,64,128]{2,1,0:T(8,128)(2,1)}), bf16[64,64,128]{2,1,0:T(8,128)(2,1)S(1)}, u32[]{:S(2)}, u32[]{:S(2)}) async-start(bf16[64,64,128]{2,1,0:T(8,128)(2,1)} %get-tuple-element.5), calls=%async_computation.1 | async-start | bytes 2097152 | tf_op jit(solution)/shard_map/all_to_all | solution.py:485
  125.3 0.0 copy-done.4
  125.3 5.0 %collective-permute-start.1 = (bf16[1280,128]{1,0:T(8,128)(2,1)S(1)}, bf16[1280,128]{1,0:T(8,128)(2,1)S(1)}, u32[]{:S(2)}, u32[]{:S(2)}) collective-permute-start(bf16[1280,128]{1,0:T(8,128)(2,1)S(1)} %copy-done.4), channel_id=1, source_target_pairs={{1,0},{2,1},{0,2},{5,4},{6,5},{4,6},{9,8},{10,9},{8,10},{13,12},{1... | collective-permute-start | bytes 983048 | tf_op jit(solution)/shard_map/ppermute | solution.py:482
  130.3 1.9 collective-permute-start.2
  132.3 0.6 copy.23
  132.9 12.1 %collective-permute-done.1.after = bf16[1280,128]{1,0:T(8,128)(2,1)S(1)} collective-permute-done((bf16[1280,128]{1,0:T(8,128)(2,1)S(1)}, bf16[1280,128]{1,0:T(8,128)(2,1)S(1)}, u32[]{:S(2)}, u32[]{:S(2)}) %collective-permute-start.1) | collective-permute-done | bytes 327712 | tf_op jit(solution)/shard_map/ppermute | solution.py:482
  144.9 0.0 copy-start.5
  144.9 5.2 %collective-permute-done.2.before = bf16[1280,128]{1,0:T(8,128)(2,1)} collective-permute-done((bf16[1280,128]{1,0:T(8,128)(2,1)S(1)}, bf16[1280,128]{1,0:T(8,128)(2,1)}, u32[]{:S(2)}, u32[]{:S(2)}) %collective-permute-start.2) | collective-permute-done | bytes 327712 | tf_op jit(solution)/shard_map/ppermute | solution.py:482
  150.1 0.0 all-to-all-done.1.sums.got
  150.1 0.0 copy-start.1
  150.1 0.0 copy-done.5
  150.1 1.0 copy-done.1
  151.1 21.9 %second_layer.1 = bf16[1280,128]{1,0:T(8,128)(2,1)} custom-call(s32[1]{0:T(128)} %bitcast.1.scal, bf16[2,32,320,128]{3,2,1,0:T(8,128)(2,1)} %bitcast.7.kv.x_rest, bf16[1280,128]{1,0:T(8,128)(2,1)} %get-tuple-element.4.own, bf16[1280,128]{1,0:T(8,128)(2,1)} %copy-done.5, bf16[1280,128]{1,0:T(8,128)(2,1)} %collective-permute-done.2.before, ...), custom_call_target="tpu_custom_call" | custom-call | tf_op jit(solution)/shard_map/second_layer/pallas_call | solution.py:377
  173.0 0.0 collective-permute-start.3
  173.0 1.8 collective-permute-done.3
  174.9 1.1 fusion.1
  176.0 0.9 broadcast_in_dim.7
  176.9 11.3 %all-to-all-start.2 = ((bf16[64,40,128]{2,1,0:T(8,128)(2,1)}), bf16[64,40,128]{2,1,0:T(8,128)(2,1)S(1)}, u32[]{:S(2)}, u32[]{:S(2)}) async-start(bf16[64,40,128]{2,1,0:T(8,128)(2,1)} %bitcast.14), calls=%async_computation.2 | async-start | bytes 1310720 | tf_op jit(solution)/shard_map/all_to_all | solution.py:494
  188.2 3.3 %home.1 = bf16[2,120,2560]{2,1,0:T(8,128)(2,1)} custom-call(s32[1]{0:T(128)} %bitcast.2.scal, bf16[64,64,128]{2,1,0:T(8,128)(2,1)} %copy-done.1, bf16[120,2560]{1,0:T(8,128)(2,1)} %stream.3, f32[8,128]{1,0:T(8,128)} %select_maximum_fusion.frames, f32[16,7680]{1,0:T(8,128)} %get-tuple-element.19.frame_mod, f32[3,2560]{1,0:T(4,128)} %bitcast.48), custom_call_target="tpu_custom_call" | custom-call | tf_op jit(solution)/shard_map/home/pallas_call | solution.py:410
  191.5 11.8 %all-to-all-done.2.got = bf16[64,40,128]{2,1,0:T(8,128)(2,1)S(1)} async-done(((bf16[64,40,128]{2,1,0:T(8,128)(2,1)}), bf16[64,40,128]{2,1,0:T(8,128)(2,1)S(1)}, u32[]{:S(2)}, u32[]{:S(2)}) %all-to-all-start.2) | async-done | bytes 655392 | tf_op jit(solution)/shard_map/all_to_all | solution.py:494
  203.3 0.0 copy-start.2
  203.3 0.8 copy-done.2
  204.1 1.9 unpack.1
  (18 shorter events, 0.3 us)
Async XLA Ops:
  0.6 28.4 %copy-start = (f32[50,7680]{1,0:T(8,128)S(1)}, f32[50,7680]{1,0:T(8,128)}, u32[]{:S(2)}) copy-start(f32[50,7680]{1,0:T(8,128)} %param.11) | copy-start | bytes 4608004
  13.5 11.9 %copy-start.8 = (f32[1,3,2560]{2,0,1:T(1,128)S(1)}, f32[1,3,2560]{2,0,1:T(1,128)}, u32[]{:S(2)}) copy-start(f32[1,3,2560]{2,0,1:T(1,128)} %param.14) | copy-start | bytes 92164
  13.5 11.9 %copy-start.6 = (f32[1,7680]{1,0:T(1,128)S(1)}, f32[1,7680]{1,0:T(1,128)}, u32[]{:S(2)}) copy-start(f32[1,7680]{1,0:T(1,128)} %param.13) | copy-start | bytes 92164
  13.5 11.9 %copy-start.7 = (f32[1,7680]{1,0:T(1,128)S(1)}, f32[1,7680]{1,0:T(1,128)}, u32[]{:S(2)}) copy-start(f32[1,7680]{1,0:T(1,128)} %param.12) | copy-start | bytes 92164
  13.5 15.5 %copy-start.9 = (s32[16]{0:T(128)S(1)}, s32[16]{0:T(128)}, u32[]{:S(2)}) copy-start(s32[16]{0:T(128)} %param.10) | copy-start | bytes 196
  13.6 78.2 %all-to-all-start = ((bf16[64,320,128]{2,1,0:T(8,128)(2,1)}), bf16[64,320,128]{2,1,0:T(8,128)(2,1)}, u32[]{:S(2)}, u32[]{:S(2)}) async-start(bf16[64,320,128]{2,1,0:T(8,128)(2,1)} %pack.1), calls=%async_computation | async-start | bytes 10485760 | tf_op jit(solution)/shard_map/all_to_all | solution.py:459
  25.5 18.0 %copy-start.3 = (f32[1,3,2560]{2,1,0:T(4,128)}, f32[1,3,2560]{2,1,0:T(4,128)S(1)}, u32[]{:S(2)}) copy-start(f32[1,3,2560]{2,1,0:T(4,128)S(1)} %copy.22) | copy-start | bytes 92164
  25.8 17.6 %collective-permute-start = (f32[6,2560]{1,0:T(8,128)S(1)}, f32[6,2560]{1,0:T(8,128)S(1)}, u32[]{:S(2)}, u32[]{:S(2)}) collective-permute-start(f32[6,2560]{1,0:T(8,128)S(1)} %pad_maximum_fusion.1), channel_id=1, source_target_pairs={{0,32},{32,0},{1,33},{33,1},{2,34},{34,2},{3,35},{35,3},{4,36},{36... | collective-permute-start | bytes 184328 | tf_op jit(solution)/shard_map/ppermute | solution.py:452
  113.9 11.4 %copy-start.4 = (bf16[1280,128]{1,0:T(8,128)(2,1)S(1)}, bf16[1280,128]{1,0:T(8,128)(2,1)}, u32[]{:S(2)}) copy-start(bf16[1280,128]{1,0:T(8,128)(2,1)} %get-tuple-element.4.own) | copy-start | bytes 983044
  113.9 36.2 %all-to-all-start.1 = ((bf16[64,64,128]{2,1,0:T(8,128)(2,1)}), bf16[64,64,128]{2,1,0:T(8,128)(2,1)S(1)}, u32[]{:S(2)}, u32[]{:S(2)}) async-start(bf16[64,64,128]{2,1,0:T(8,128)(2,1)} %get-tuple-element.5), calls=%async_computation.1 | async-start | bytes 2097152 | tf_op jit(solution)/shard_map/all_to_all | solution.py:485
  125.3 19.6 %collective-permute-start.1 = (bf16[1280,128]{1,0:T(8,128)(2,1)S(1)}, bf16[1280,128]{1,0:T(8,128)(2,1)S(1)}, u32[]{:S(2)}, u32[]{:S(2)}) collective-permute-start(bf16[1280,128]{1,0:T(8,128)(2,1)S(1)} %copy-done.4), channel_id=1, source_target_pairs={{1,0},{2,1},{0,2},{5,4},{6,5},{4,6},{9,8},{10,9},{8,10},{13,12},{1... | collective-permute-start | bytes 983048 | tf_op jit(solution)/shard_map/ppermute | solution.py:482
  130.3 19.8 %collective-permute-start.2 = (bf16[1280,128]{1,0:T(8,128)(2,1)S(1)}, bf16[1280,128]{1,0:T(8,128)(2,1)}, u32[]{:S(2)}, u32[]{:S(2)}) collective-permute-start(bf16[1280,128]{1,0:T(8,128)(2,1)S(1)} %copy-done.4), channel_id=1, source_target_pairs={{2,0},{0,1},{1,2},{6,4},{4,5},{5,6},{10,8},{8,9},{9,10},{14,12},{1... | collective-permute-start | bytes 983048 | tf_op jit(solution)/shard_map/ppermute | solution.py:482
  144.9 5.2 %copy-start.5 = (bf16[1280,128]{1,0:T(8,128)(2,1)}, bf16[1280,128]{1,0:T(8,128)(2,1)S(1)}, u32[]{:S(2)}) copy-start(bf16[1280,128]{1,0:T(8,128)(2,1)S(1)} %collective-permute-done.1.after) | copy-start | bytes 983044
  150.1 1.0 copy-start.1
  173.0 1.8 collective-permute-start.3
  176.9 26.3 %all-to-all-start.2 = ((bf16[64,40,128]{2,1,0:T(8,128)(2,1)}), bf16[64,40,128]{2,1,0:T(8,128)(2,1)S(1)}, u32[]{:S(2)}, u32[]{:S(2)}) async-start(bf16[64,40,128]{2,1,0:T(8,128)(2,1)} %bitcast.14), calls=%async_computation.2 | async-start | bytes 1310720 | tf_op jit(solution)/shard_map/all_to_all | solution.py:494
  203.3 0.8 copy-start.2

commit v2 on v1

--- a/solution.py
+++ b/solution.py
@@ -26,7 +26,8 @@
 PARAMS = pltpu.CompilerParams(vmem_limit_bytes=VMEM_BYTES)
 
 OWN_ROWS = PATCHES * THIRD
-TILE = 4 * THIRD
+TILE = 640
+FACTOR = HEAD_DIM ** (-0.5) * math.log2(math.e)
 CHUNK = 320
 MID = 64
 
@@ -58,68 +59,70 @@
     return rows if cut == 0 else jnp.concatenate([rows[cut:TOK], rows[:cut]], axis=0)
 
 
-def pack_kernel(scal, kv, kv_more, x, x_more, stream, frames, out, aux):
+def pack_kernel(scal, stale, stream, frames, out, aux, frame_row):
     step = pl.program_id(0)
     section = scal[0]
 
     @pl.when(step == 0)
     def _():
-        values = stream[...].astype(F32)
-        square = values * values
-        ones = jnp.ones((8, WIDTH), BF16)
+        frame_row[...] = jnp.zeros((8, 128), F32)
+        frame_row[0:1, 0:TOK] = frames[...].astype(F32)
+        square = jnp.zeros((TOK, 128), F32)
+        for head in range(HEADS):
+            part = stream[:, 128 * head : 128 * head + 128].astype(F32)
+            square = square + part * part
+        square = jnp.concatenate([square, jnp.zeros((8, 128), F32)], axis=0)
+        total = jnp.sum(square.T, axis=0, keepdims=True)
+        r = lax.rsqrt(total * (1.0 / WIDTH) + EPSILON)
+        hi, mid, low = split3(jnp.broadcast_to(r, (8, 128)))
         row = lax.broadcasted_iota(jnp.int32, (8, 128), 0)
         lane = lax.broadcasted_iota(jnp.int32, (8, 128), 1)
+        a = jnp.where(row == 0, hi, jnp.where(row == 1, mid, jnp.where(row == 2, low, 0.0)))
+        a = jnp.where(row == 3, frame_row[0:1, :], a)
+        a = jnp.where(lane < TOK, a, 0.0)
+        aux[0] = a
+        for third in range(1, 3):
+            cut = THIRD * third
+            t = jnp.where(lane < TOK - cut, pltpu.roll(a, 128 - cut, 1), pltpu.roll(a, TOK - cut, 1))
+            aux[third] = jnp.where(lane < TOK, t, 0.0)
+
+    none = jnp.zeros((8, 128), F32)
+
+    def blocks(head):
+        cols = pl.ds(pl.multiple_of(head * 128, 128), 128)
+        keys = stale[0, :, cols].astype(F32)
+        vals = jnp.concatenate([stale[1, :, cols].astype(F32), none], axis=0).T.astype(BF16)
+        x = stream[:, cols].astype(F32)
+        halves = []
         for third in range(3):
-            t = jnp.concatenate([turned(square, third), jnp.zeros((8, WIDTH), F32)], axis=0)
-            hi = t.astype(BF16)
-            low = (t - hi.astype(F32)).astype(BF16)
-            total = dot(ones, hi, NT) + dot(ones, low, NT)
-            r = jnp.where(lane < TOK, lax.rsqrt(total * (1.0 / WIDTH) + EPSILON), 0.0)
-            hi, mid, low = split3(r)
-            a = jnp.where(row == 0, hi, jnp.where(row == 1, mid, jnp.where(row == 2, low, 0.0)))
-            aux[third] = jnp.where(row == 3, frames[third : third + 1, :], a)
-
-    def halves(block):
-        values = block[...].astype(F32)
-        parts = []
+            t = turned(x, third)
+            halves.append(jnp.where(section == 0, t[0:64], t[TOK - 64 : TOK]).astype(BF16))
+        return keys, vals, halves
+
+    def put(at, keys, vals, x, third):
+        out[at, 0:128] = jnp.concatenate([keys, aux[third]], axis=0).astype(BF16)
+        out[at, 128:256] = vals
+        out[at, 256:CHUNK] = x
+
+    more_keys, more_vals, more_x = blocks(16 + step)
+    for y in range(4):
+        keys, vals, halves = blocks(4 * step + y)
         for third in range(3):
-            t = turned(values, third)
-            parts.append(jnp.where(section == 0, t[0:64], t[TOK - 64 : TOK]))
-        return parts
-
-    none = jnp.zeros((8, 128), F32)
-    keys = kv[0].astype(F32)
-    vals = jnp.concatenate([kv[1].astype(F32), none], axis=0).astype(BF16)
-    xs = halves(x)
-    for third in range(3):
-        out[third, 0:128] = jnp.concatenate([keys, aux[third]], axis=0).astype(BF16)
-        out[third, 128:256] = vals
-        out[third, 256:CHUNK] = xs[third].astype(BF16)
-    y = lax.rem(step, 4)
-    keys = kv_more[0].astype(F32)
-    vals = jnp.concatenate([kv_more[1].astype(F32), none], axis=0).astype(BF16)
-    xs = halves(x_more)
-    which = jnp.where(y == 3, 0, y)
-    out[3, 0:128] = jnp.concatenate([keys, aux[which]], axis=0).astype(BF16)
-    out[3, 128:256] = vals
-    chosen = jnp.where(which == 0, xs[0], jnp.where(which == 1, xs[1], xs[2]))
-    out[3, 256:CHUNK] = chosen.astype(BF16)
+            put(4 * y + third, keys, vals, halves[third], third)
+        put(4 * y + 3, more_keys, more_vals, more_x[y % 3], y % 3)
 
 
 def pack(section, stale, stream, frames):
     grid = pltpu.PrefetchScalarGridSpec(
         num_scalar_prefetch=1,
-        grid=(16,),
+        grid=(4,),
         in_specs=[
-            pl.BlockSpec((2, TOK, 128), lambda r, s: (0, 0, r)),
-            pl.BlockSpec((2, TOK, 128), lambda r, s: (0, 0, 16 + r // 4)),
-            pl.BlockSpec((TOK, 128), lambda r, s: (0, r)),
-            pl.BlockSpec((TOK, 128), lambda r, s: (0, 16 + r // 4)),
+            pl.BlockSpec((2, TOK, WIDTH), lambda r, s: (0, 0, 0)),
             pl.BlockSpec((TOK, WIDTH), lambda r, s: (0, 0)),
-            pl.BlockSpec((8, 128), lambda r, s: (0, 0)),
+            pl.BlockSpec((1, TOK), lambda r, s: (0, 0)),
         ],
-        out_specs=pl.BlockSpec((4, CHUNK, 128), lambda r, s: (r, 0, 0)),
-        scratch_shapes=[pltpu.VMEM((3, 8, 128), F32)],
+        out_specs=pl.BlockSpec((16, CHUNK, 128), lambda r, s: (r, 0, 0)),
+        scratch_shapes=[pltpu.VMEM((3, 8, 128), F32), pltpu.VMEM((8, 128), F32)],
     )
     return pl.pallas_call(
         pack_kernel,
@@ -127,7 +130,7 @@
         out_shape=jax.ShapeDtypeStruct((64, CHUNK, 128), BF16),
         compiler_params=PARAMS,
         name="pack",
-    )(section, stale, stale, stream, stream, stream, frames)
+    )(section, stale, stream, frames)
 
 
 def mod_table(frame_mod, with_scale):
@@ -146,81 +149,83 @@
     return jnp.concatenate([hot, aux, jnp.zeros((8, 128), F32)], axis=0).astype(BF16)
 
 
-def place_keys(p, kv, ka, va):
+def place_keys(p, kv, ka, vt):
     row = lax.broadcasted_iota(jnp.int32, (128, 128), 0)
     col = lax.broadcasted_iota(jnp.int32, (128, 128), 1)
     at = pl.ds(pl.multiple_of(p * 128, 128), 128)
     hidden = (col == p) | ((col == PATCHES) & (row >= TOK))
     ka[at, 0:128] = kv[0, p, 0:128, :]
     ka[at, 128:256] = jnp.where(hidden, -BIG, 0.0).astype(BF16)
-    va[at, 0:128] = kv[0, p, 128:256, :]
-    va[at, 128:256] = jnp.ones((128, 128), BF16)
-
-
-def place_fresh(p, hid, maps, fk, fv):
-    row = lax.broadcasted_iota(jnp.int32, (128, 128), 0)
-    col = lax.broadcasted_iota(jnp.int32, (128, 128), 1)
-    at = pl.ds(pl.multiple_of(p * 128, 128), 128)
-    fk[at, 0:128] = (hid * maps[1:2, :]).astype(BF16)
-    fk[at, 128:256] = jnp.where((col == PATCHES) & (row >= TOK), -BIG, 0.0).astype(BF16)
-    fv[at, 0:128] = (hid * maps[2:3, :]).astype(BF16)
-    fv[at, 128:256] = jnp.ones((128, 128), BF16)
-
-
-def place_query(t, pair_hid, maps, qa):
+    vt[0:128, at] = kv[0, p, 128:256, :]
+    vt[128:144, at] = jnp.ones((16, 128), BF16)
+
+
+def place_pair(t, hids, maps, qa, of, mf):
     row = lax.broadcasted_iota(jnp.int32, (80, 128), 0)
     col = lax.broadcasted_iota(jnp.int32, (80, 128), 1)
     patch = 2 * t + jnp.where(row >= THIRD, 1, 0)
     at = pl.ds(pl.multiple_of(t * 80, 16), 80)
-    qa[at, 0:128] = (pair_hid * maps[0:1, :]).astype(BF16)
+    q = (jnp.concatenate([hid[0:THIRD] for hid in hids], axis=0) * maps[0:1, :]).astype(BF16)
+    qa[at, 0:128] = q
     qa[at, 128:256] = jnp.where((col == patch) | (col == PATCHES), 1.0, 0.0).astype(BF16)
-
-
-def attention(qa, ka, va, fk, fv, xo, go, sc, pc, result):
-    factor = HEAD_DIM ** (-0.5) * math.log2(math.e)
-    keys = ka.shape[0]
+    keys = jnp.concatenate([(hid * maps[1:2, :]).astype(BF16) for hid in hids], axis=0)
+    vals = jnp.concatenate([(hid * maps[2:3, :]).astype(BF16) for hid in hids], axis=0)
+    s = dot(q, keys, NT)
+    s = jnp.concatenate([s[0:THIRD, 0:128], s[THIRD:80, 128:256]], axis=0)
+    s = jnp.where(col < TOK, s, -BIG)
+    top = jnp.max(s, axis=1, keepdims=True)
+    power = jnp.exp2((s - top) * FACTOR)
+    none = jnp.zeros((THIRD, 128), F32)
+    both = [
+        jnp.concatenate([power[0:THIRD], none], axis=1),
+        jnp.concatenate([none, power[THIRD:80]], axis=1),
+    ]
+    both = jnp.concatenate(both, axis=0).astype(BF16)
+    vals = jnp.concatenate([vals, jnp.ones((256, 128), BF16)], axis=1)
+    of[at, :] = dot(both, vals, NN)
+    mf[at, :] = jnp.broadcast_to(top, (80, 128))
+
+
+def attention(qa, ka, vt, of, mf, xo, go, sc, pt, result):
     step = 512
-
-    @pl.loop(0, OWN_ROWS // TILE)
-    def _(tile):
-        at = pl.ds(pl.multiple_of(tile * TILE, 16), TILE)
-        q = qa[at, :]
-        top = None
-        for begin in range(0, keys, step):
-            s = dot(q, ka[begin : begin + step, :], NT)
-            sc[:, begin : begin + step] = s
-            for lane in range(0, step, 128):
-                part = s[:, lane : lane + 128]
-                top = part if top is None else jnp.maximum(top, part)
-        fresh = []
-        for pair in range(2):
-            low = pl.multiple_of(tile * TILE + pair * 80, 16)
-            klow = pl.multiple_of((tile * 4 + pair * 2) * 128, 256)
-            s = dot(qa[pl.ds(low, 80), :], fk[pl.ds(klow, 256), :], NT)
-            fresh.append(s[0:THIRD, 0:128])
-            fresh.append(s[THIRD:80, 128:256])
-        fresh = jnp.concatenate(fresh, axis=0)
-        top = jnp.max(jnp.maximum(top, fresh), axis=1, keepdims=True)
-        for begin in range(0, keys, step):
-            pc[:, begin : begin + step] = jnp.exp2((sc[:, begin : begin + step] - top) * factor).astype(BF16)
-        total = dot(pc[...], va[...], NN)
-        power = jnp.exp2((fresh - top) * factor)
-        none = jnp.zeros((THIRD, 128), F32)
-        added = []
-        for pair in range(2):
-            a = power[pair * 80 : pair * 80 + THIRD]
-            b = power[pair * 80 + THIRD : pair * 80 + 80]
-            both = jnp.concatenate(
-                [jnp.concatenate([a, none], axis=1), jnp.concatenate([none, b], axis=1)], axis=0
-            ).astype(BF16)
-            klow = pl.multiple_of((tile * 4 + pair * 2) * 128, 256)
-            added.append(dot(both, fv[pl.ds(klow, 256), :], NN))
-        total = total + jnp.concatenate(added, axis=0)
-        attended = total[:, 0:128] / total[:, 128:256]
+    begins = range(0, PATCHES * 128, step)
+    tiles = OWN_ROWS // TILE
+    tops = [None] * tiles
+
+    def score(tile, begin):
+        s = dot(ka[begin : begin + step, :], qa[tile * TILE : tile * TILE + TILE, :], NT)
+        sc[tile % 2, begin : begin + step, :] = s
+        top = jnp.max(s.reshape(step // 8, 8, TILE), axis=0)
+        tops[tile] = top if begin == 0 else jnp.maximum(tops[tile], top)
+
+    def weigh(tile, begin, top):
+        s = sc[tile % 2, begin : begin + step, :]
+        pt[tile % 2, begin : begin + step, :] = jnp.exp2((s - top) * FACTOR).astype(BF16)
+
+    def finish(tile, top):
+        total = dot(vt[...], pt[tile % 2], NN)
+        own = total[0:128].T
+        stats = jnp.concatenate([total[128:136], jnp.broadcast_to(top, (8, TILE))], axis=0).T
+        at = slice(tile * TILE, tile * TILE + TILE)
+        top_s, top_f = stats[:, 8:9], mf[at, 0:1]
+        top = jnp.maximum(top_s, top_f)
+        a, b = jnp.exp2((top_s - top) * FACTOR), jnp.exp2((top_f - top) * FACTOR)
+        fresh = of[at, :]
+        attended = (a * own + b * fresh[:, 0:128]) / (a * stats[:, 0:1] + b * fresh[:, 128:256])
         result(at, (xo[at, :] + go[at, :] * attended).astype(BF16))
 
-
-def first_kernel(kv, x_rest, frame_mod, maps, x_out, mid, qa, ka, va, fk, fv, xo, go, sc, pc, sq):
+    for begin in begins:
+        score(0, begin)
+    for tile in range(tiles):
+        top = jnp.max(tops[tile], axis=0, keepdims=True)
+        for begin in begins:
+            if tile + 1 < tiles:
+                score(tile + 1, begin)
+            weigh(tile, begin, top)
+        finish(tile, top)
+
+
+def first_kernel(kv, x_rest, frame_mod, maps, x_out, sums, qa, ka, vt, of, mf, xo, go, sc, pt, sq):
     table = mod_table(frame_mod[...], True)
     gains = maps[...]
 
@@ -237,12 +242,11 @@
                 x = jnp.concatenate([xa, xb, jnp.zeros((8, 128), F32)], axis=0)
                 m = dot(hot_rows(aux), table, TN)
                 hid = x * m[:, 384:512] * (1.0 + m[:, 128:256]) + m[:, 0:128]
-                place_keys(p, kv, ka, va)
-                place_fresh(p, hid, gains, fk, fv)
-                hids.append(hid[0:THIRD])
+                place_keys(p, kv, ka, vt)
+                hids.append(hid)
                 xs.append(x[0:THIRD])
                 gates.append(m[0:THIRD, 256:384])
-            place_query(t, jnp.concatenate(hids, axis=0), gains, qa)
+            place_pair(t, hids, gains, qa, of, mf)
             at = pl.ds(pl.multiple_of(t * 80, 16), 80)
             xo[at, :] = jnp.concatenate(xs, axis=0)
             go[at, :] = jnp.concatenate(gates, axis=0)
@@ -252,18 +256,22 @@
         wide = value.astype(F32)
         sq[at, :] = wide * wide
 
-    attention(qa, ka, va, fk, fv, xo, go, sc, pc, result)
+    attention(qa, ka, vt, of, mf, xo, go, sc, pt, result)
     square = sq[...]
     hi = square.astype(BF16)
     low = (square - hi.astype(F32)).astype(BF16)
     ones = jnp.ones((8, 128), BF16)
     total = dot(ones, hi, NT) + dot(ones, low, NT)
-    hi = total.astype(BF16).astype(F32)
-    low = total - hi
+    sums[...] = total
+
+
+def mid_kernel(x, total, mid):
+    hi = total[...].astype(BF16).astype(F32)
+    low = total[...] - hi
     rows = [part[0:1, 128 * i : 128 * i + 128] for part in (hi, low) for i in range(10)]
     sums = jnp.concatenate(rows + [jnp.zeros((4, 128), F32)], axis=0)
     for t in range(PATCHES // 2):
-        pair = x_out[80 * t : 80 * t + 80, :].astype(F32)
+        pair = x[80 * t : 80 * t + 80, :].astype(F32)
         for half in range(2):
             p = 2 * t + half
             block = jnp.concatenate([pair[THIRD * half : THIRD * half + THIRD], sums], axis=0).astype(BF16)
@@ -271,16 +279,28 @@
             mid[PATCHES + p] = block
 
 
+def middle(x, total):
+    whole = pl.BlockSpec(memory_space=pltpu.VMEM)
+    return pl.pallas_call(
+        mid_kernel,
+        in_specs=[whole, whole],
+        out_specs=whole,
+        out_shape=jax.ShapeDtypeStruct((64, MID, 128), BF16),
+        compiler_params=PARAMS,
+        name="middle",
+    )(x, total)
+
+
 SCRATCH = [
     pltpu.VMEM((OWN_ROWS, 256), BF16),
     pltpu.VMEM((PATCHES * 128, 256), BF16),
-    pltpu.VMEM((PATCHES * 128, 256), BF16),
-    pltpu.VMEM((PATCHES * 128, 256), BF16),
-    pltpu.VMEM((PATCHES * 128, 256), BF16),
+    pltpu.VMEM((144, PATCHES * 128), BF16),
+    pltpu.VMEM((OWN_ROWS, 256), F32),
     pltpu.VMEM((OWN_ROWS, 128), F32),
     pltpu.VMEM((OWN_ROWS, 128), F32),
-    pltpu.VMEM((TILE, PATCHES * 128), F32),
-    pltpu.VMEM((TILE, PATCHES * 128), BF16),
+    pltpu.VMEM((OWN_ROWS, 128), F32),
+    pltpu.VMEM((2, PATCHES * 128, TILE), F32),
+    pltpu.VMEM((2, PATCHES * 128, TILE), BF16),
 ]
 
 
@@ -296,11 +316,11 @@
         ],
         out_specs=[
             pl.BlockSpec((OWN_ROWS, 128), lambda i: (0, 0)),
-            pl.BlockSpec((64, MID, 128), lambda i: (0, 0, 0)),
+            pl.BlockSpec((8, OWN_ROWS), lambda i: (0, 0)),
         ],
         out_shape=[
             jax.ShapeDtypeStruct((OWN_ROWS, 128), BF16),
-            jax.ShapeDtypeStruct((64, MID, 128), BF16),
+            jax.ShapeDtypeStruct((8, OWN_ROWS), F32),
         ],
         scratch_shapes=SCRATCH + [pltpu.VMEM((OWN_ROWS, 128), F32)],
         compiler_params=PARAMS,
@@ -308,7 +328,7 @@
     )(received, received, frame_mod, maps)
 
 
-def second_kernel(scal, kv, own, after, before, sums, frame_mod, maps, x_out, qa, ka, va, fk, fv, xo, go, sc, pc, rs):
+def second_kernel(scal, kv, own, after, before, sums, frame_mod, maps, x_out, qa, ka, vt, of, mf, xo, go, sc, pt, rs):
     table = mod_table(frame_mod[...], False)
     gains = maps[...]
     third = scal[0]
@@ -343,18 +363,17 @@
                 r = jnp.concatenate([v[cut] for v in scale] + none, axis=0)
                 m = dot(hot_rows(aux), table, TN)
                 hid = x * r * (1.0 + m[:, 128:256]) + m[:, 0:128]
-                place_keys(p, kv, ka, va)
-                place_fresh(p, hid, gains, fk, fv)
-                hids.append(hid[0:THIRD])
+                place_keys(p, kv, ka, vt)
+                hids.append(hid)
                 gates.append(m[0:THIRD, 256:384])
-            place_query(t, jnp.concatenate(hids, axis=0), gains, qa)
+            place_pair(t, hids, gains, qa, of, mf)
             xo[at, :] = pair[0]
             go[at, :] = jnp.concatenate(gates, axis=0)
 
     def result(at, value):
         x_out[at, :] = value
 
-    attention(qa, ka, va, fk, fv, xo, go, sc, pc, result)
+    attention(qa, ka, vt, of, mf, xo, go, sc, pt, result)
 
 
 def second_layer(third, received, own, after, before, sums, frame_mod, maps):
@@ -383,8 +402,9 @@
     )(third, received, own, after, before, sums, frame_mod, maps)
 
 
-def home_kernel(scal, got, stream, frames, frame_mod, maps, out, xs):
+def home_kernel(scal, got, stream, frames, frame_mod, maps, out, xs, frame_row):
     section = scal[0]
+    frame_row[0:1, 0:TOK] = frames[...].astype(F32)
     square = jnp.zeros((TOK, 128), F32)
     for head in range(HEADS):
         cols = slice(128 * head, 128 * head + 128)
@@ -394,7 +414,7 @@
         square = square + x * x
     r = lax.rsqrt(jnp.sum(square, axis=1, keepdims=True) * (1.0 / WIDTH) + EPSILON)
     row = lax.broadcasted_iota(jnp.int32, (48, 128), 0)
-    hot = jnp.where((row & 15).astype(F32) == frames[0:1, :], 1.0, 0.0).astype(BF16)
+    hot = jnp.where((row & 15).astype(F32) == frame_row[0:1, :], 1.0, 0.0).astype(BF16)
     for head in range(HEADS):
         cols = slice(128 * head, 128 * head + 128)
         more = slice(WIDTH + 128 * head, WIDTH + 128 * head + 128)
@@ -412,7 +432,7 @@
         in_specs=[pl.BlockSpec(memory_space=pltpu.SMEM)] + [whole] * 5,
         out_specs=whole,
         out_shape=jax.ShapeDtypeStruct((2, TOK, WIDTH), BF16),
-        scratch_shapes=[pltpu.VMEM((TOK, WIDTH), F32)],
+        scratch_shapes=[pltpu.VMEM((TOK, WIDTH), F32), pltpu.VMEM((8, 128), F32)],
         compiler_params=PARAMS,
         name="home",
     )(section, got, stream, frames, frame_mod, maps)
@@ -451,9 +471,7 @@
     both = jnp.concatenate([layer_mod.reshape(3, WIDTH), maps[0]], axis=0)
     other = lax.ppermute(both, "section", [(0, 1), (1, 0)])
 
-    tf = token_frame.astype(F32)
-    frames = jnp.stack([jnp.pad(jnp.roll(tf, -THIRD * k), (0, 8), constant_values=-1.0) for k in range(3)])
-    frames = jnp.pad(frames, ((0, 5), (0, 0)))
+    frames = token_frame.reshape(1, TOK)
     section_at = section.reshape(1).astype(jnp.int32)
     send = pack(section_at, stale_kv[0, 0], stream, frames)
     received = lax.all_to_all(send, PLANE, 0, 0, tiled=True)
@@ -475,13 +493,14 @@
     mods = mods.reshape(2, FRAMES, 384)
     gains = mine[:, 3:6]
 
-    x_one, mid = first_layer(received, mods[0], gains[0])
+    x_one, total = first_layer(received, mods[0], gains[0])
 
     def from_third(by):
         pairs = [(place_of(h, (g + by) % 3), place_of(h, g)) for h in range(HEADS) for g in range(3)]
         return lax.ppermute(x_one, PLANE, pairs)
 
     after, before = from_third(1), from_third(2)
+    mid = middle(x_one, total)
     mid_got = lax.all_to_all(mid, PLANE, 0, 0, tiled=True)
     fresh = home(section_at, mid_got, stream, frames, home_mod, maps[0])
     x_two = second_layer(third.reshape(1).astype(jnp.int32), received, x_one, after, before, mid_got, mods[1], gains[1])

time: 207 us -> 198 us (0.957)
  Pallas kernels: 60.5 us -> 53.7 us
    pallas_call x1, Pallas kernels: 11.3 us -> 4.95 us  [pack(): pl.pallas_call(pack_kernel, grid_spec=grid, out_shape=jax.ShapeDtypeStruc...]
    pallas_call x0 -> x1, Pallas kernels: none -> 2.14 us  [middle(): pl.pallas_call(mid_kernel, in_specs=[whole, whole], out_specs=whole, out_...]
where the time goes in v2:
time: 198 us
  waiting for transfers between devices  90.3 us (46%)
  Pallas kernels  53.7 us (27%)
  starting transfers between devices  44.8 us (23%)
  local copies, waits for them, and re-layouts  4.88 us (2%)
    all_to_all x1, waiting for transfers between devices, body(): received = lax.all_to_all(send, PLANE, 0, 0, tiled=True)  46.9 us
    pallas_call x1, Pallas kernels, first_layer(): pl.pallas_call(first_kernel, grid=(1,), in_specs=[pl.BlockSpec((1, PATCHE...  20.9 us
    pallas_call x1, Pallas kernels, second_layer(): pl.pallas_call(second_kernel, grid_spec=grid, out_shape=jax.ShapeDtypeStr...  20.6 us
    ppermute x2, waiting for transfers between devices, from_third(): return lax.ppermute(x_one, PLANE, pairs)  17 us
    ppermute x1, waiting for transfers between devices, body(): other = lax.ppermute(both, 'section', [(0, 1), (1, 0)])  12.8 us
    all_to_all x1, starting transfers between devices, body(): received = lax.all_to_all(send, PLANE, 0, 0, tiled=True)  11.9 us
    all_to_all x1, waiting for transfers between devices, body(): guided_got = lax.all_to_all(guided, PLANE, 0, 0, tiled=True)  11.8 us
    all_to_all x1, starting transfers between devices, body(): guided_got = lax.all_to_all(guided, PLANE, 0, 0, tiled=True)  11.3 us
  transfers between devices with their start and end apart: 7, of which 6 were waited for; matrix products, arithmetic and copies ran while one was open for 2% of the time, Pallas kernels for 2%

profile of v2, /device:TPU:0, one launch (start us, length us, event | category | flops | bytes accessed | tf_op | source)
XLA Modules:
  0.0 197.5 jit_solution(5385705010207849074)
XLA Ops:
  0.6 0.0 copy-start
  0.7 4.9 %pack.1 = bf16[64,320,128]{2,1,0:T(8,128)(2,1)} custom-call(s32[1]{0:T(128)} %bitcast.2.scal, bf16[2,120,2560]{2,1,0:T(8,128)(2,1)} %bitcast.39, bf16[120,2560]{1,0:T(8,128)(2,1)} %stream.3, s32[1,120]{1,0:T(1,128)} %bitcast.49), custom_call_target="tpu_custom_call" | custom-call | tf_op jit(solution)/shard_map/pack/pallas_call | solution.py:127
  5.6 0.0 copy-start.8
  5.6 0.0 copy-start.6
  5.6 0.0 copy-start.7
  5.6 0.0 copy-start.9
  5.6 11.9 %all-to-all-start = ((bf16[64,320,128]{2,1,0:T(8,128)(2,1)}), bf16[64,320,128]{2,1,0:T(8,128)(2,1)}, u32[]{:S(2)}, u32[]{:S(2)}) async-start(bf16[64,320,128]{2,1,0:T(8,128)(2,1)} %pack.1), calls=%async_computation | async-start | bytes 10485760 | tf_op jit(solution)/shard_map/all_to_all | solution.py:477
  17.5 0.0 copy-done.8
  17.5 0.0 copy-done.6
  17.5 0.0 copy-done.7
  17.5 0.0 copy-start.4
  17.6 0.2 add_reduce_fusion
  17.8 3.2 %collective-permute-start = (f32[6,2560]{1,0:T(8,128)S(1)}, f32[6,2560]{1,0:T(8,128)S(1)}, u32[]{:S(2)}, u32[]{:S(2)}) collective-permute-start(f32[6,2560]{1,0:T(8,128)S(1)} %pad_maximum_fusion.1), channel_id=1, source_target_pairs={{0,32},{32,0},{1,33},{33,1},{2,34},{34,2},{3,35},{35,3},{4,36},{36... | collective-permute-start | bytes 184328 | tf_op jit(solution)/shard_map/ppermute | solution.py:472
  21.1 0.0 copy-done
  21.1 0.0 copy-done.9
  21.1 1.5 broadcast_add_fusion
  22.6 0.1 reshape.47
  22.7 12.8 %collective-permute-done = f32[6,2560]{1,0:T(8,128)S(1)} collective-permute-done((f32[6,2560]{1,0:T(8,128)S(1)}, f32[6,2560]{1,0:T(8,128)S(1)}, u32[]{:S(2)}, u32[]{:S(2)}) %collective-permute-start) | collective-permute-done | bytes 61472 | tf_op jit(solution)/shard_map/ppermute | solution.py:472
  35.5 0.0 copy-done.4
  35.7 0.6 copy.24
  36.3 0.6 slice_bitcast_fusion
  36.9 46.9 %all-to-all-done = bf16[64,320,128]{2,1,0:T(8,128)(2,1)} async-done(((bf16[64,320,128]{2,1,0:T(8,128)(2,1)}), bf16[64,320,128]{2,1,0:T(8,128)(2,1)}, u32[]{:S(2)}, u32[]{:S(2)}) %all-to-all-start) | async-done | bytes 5242912 | tf_op jit(solution)/shard_map/all_to_all | solution.py:477
  83.8 20.9 %first_layer.1 = (bf16[1280,128]{1,0:T(8,128)(2,1)}, f32[8,1280]{1,0:T(8,128)}) custom-call(bf16[2,32,320,128]{3,2,1,0:T(8,128)(2,1)} %bitcast.5.kv.x_rest, bf16[2,32,320,128]{3,2,1,0:T(8,128)(2,1)} %bitcast.5.kv.x_rest, f32[16,384]{1,0:T(8,128)} %bitcast.46, f32[3,128]{1,0:T(4,128)} %get-tuple-element.14.maps), custom_call_target="tpu_custom_call" | custom-call | tf_op jit(solution)/shard_map/first_layer/pallas_call | solution.py:308
  104.7 0.0 copy-start.3
  104.7 2.1 %middle.1 = bf16[64,64,128]{2,1,0:T(8,128)(2,1)} custom-call(bf16[1280,128]{1,0:T(8,128)(2,1)} %get-tuple-element.4.x.own, f32[8,1280]{1,0:T(8,128)} %get-tuple-element.5.total), custom_call_target="tpu_custom_call" | custom-call | tf_op jit(solution)/shard_map/middle/pallas_call | solution.py:284
  106.9 11.3 %all-to-all-start.1 = ((bf16[64,64,128]{2,1,0:T(8,128)(2,1)}), bf16[64,64,128]{2,1,0:T(8,128)(2,1)S(1)}, u32[]{:S(2)}, u32[]{:S(2)}) async-start(bf16[64,64,128]{2,1,0:T(8,128)(2,1)} %middle.1), calls=%async_computation.1 | async-start | bytes 2097152 | tf_op jit(solution)/shard_map/all_to_all | solution.py:504
  118.1 0.0 copy-done.3
  118.2 5.2 %collective-permute-start.1 = (bf16[1280,128]{1,0:T(8,128)(2,1)S(1)}, bf16[1280,128]{1,0:T(8,128)(2,1)S(1)}, u32[]{:S(2)}, u32[]{:S(2)}) collective-permute-start(bf16[1280,128]{1,0:T(8,128)(2,1)S(1)} %copy-done.3), channel_id=1, source_target_pairs={{1,0},{2,1},{0,2},{5,4},{6,5},{4,6},{9,8},{10,9},{8,10},{13,12},{1... | collective-permute-start | bytes 983048 | tf_op jit(solution)/shard_map/ppermute | solution.py:500
  123.4 1.9 collective-permute-start.2
  125.3 0.6 copy.23
  125.9 11.8 %collective-permute-done.1.after = bf16[1280,128]{1,0:T(8,128)(2,1)S(1)} collective-permute-done((bf16[1280,128]{1,0:T(8,128)(2,1)S(1)}, bf16[1280,128]{1,0:T(8,128)(2,1)S(1)}, u32[]{:S(2)}, u32[]{:S(2)}) %collective-permute-start.1) | collective-permute-done | bytes 327712 | tf_op jit(solution)/shard_map/ppermute | solution.py:500
  137.8 0.0 copy-start.5
  137.8 5.2 %collective-permute-done.2.before = bf16[1280,128]{1,0:T(8,128)(2,1)} collective-permute-done((bf16[1280,128]{1,0:T(8,128)(2,1)S(1)}, bf16[1280,128]{1,0:T(8,128)(2,1)}, u32[]{:S(2)}, u32[]{:S(2)}) %collective-permute-start.2) | collective-permute-done | bytes 327712 | tf_op jit(solution)/shard_map/ppermute | solution.py:500
  142.9 0.0 all-to-all-done.1.sums.got
  142.9 0.0 copy-start.1
  142.9 0.0 copy-done.5
  142.9 1.0 copy-done.1
  144.0 20.6 %second_layer.1 = bf16[1280,128]{1,0:T(8,128)(2,1)} custom-call(s32[1]{0:T(128)} %bitcast.1.scal, bf16[2,32,320,128]{3,2,1,0:T(8,128)(2,1)} %bitcast.5.kv.x_rest, bf16[1280,128]{1,0:T(8,128)(2,1)} %get-tuple-element.4.x.own, bf16[1280,128]{1,0:T(8,128)(2,1)} %copy-done.5, bf16[1280,128]{1,0:T(8,128)(2,1)} %collective-permute-done.2.before, ...), custom_call_target="tpu_custom_call" | custom-call | tf_op jit(solution)/shard_map/second_layer/pallas_call | solution.py:396
  164.5 0.0 collective-permute-start.3
  164.5 1.8 collective-permute-done.3
  166.4 1.1 fusion.1
  167.5 0.9 broadcast_in_dim.7
  168.4 11.3 %all-to-all-start.2 = ((bf16[64,40,128]{2,1,0:T(8,128)(2,1)}), bf16[64,40,128]{2,1,0:T(8,128)(2,1)S(1)}, u32[]{:S(2)}, u32[]{:S(2)}) async-start(bf16[64,40,128]{2,1,0:T(8,128)(2,1)} %bitcast.12), calls=%async_computation.2 | async-start | bytes 1310720 | tf_op jit(solution)/shard_map/all_to_all | solution.py:513
  179.7 3.3 %home.1 = bf16[2,120,2560]{2,1,0:T(8,128)(2,1)} custom-call(s32[1]{0:T(128)} %bitcast.2.scal, bf16[64,64,128]{2,1,0:T(8,128)(2,1)} %copy-done.1, bf16[120,2560]{1,0:T(8,128)(2,1)} %stream.3, s32[1,120]{1,0:T(1,128)} %bitcast.50, f32[16,7680]{1,0:T(8,128)} %get-tuple-element.15.frame_mod, f32[3,2560]{1,0:T(4,128)} %bitcast.42), custom_call_target="tpu_custom_call" | custom-call | tf_op jit(solution)/shard_map/home/pallas_call | solution.py:430
  183.0 11.8 %all-to-all-done.2.got = bf16[64,40,128]{2,1,0:T(8,128)(2,1)S(1)} async-done(((bf16[64,40,128]{2,1,0:T(8,128)(2,1)}), bf16[64,40,128]{2,1,0:T(8,128)(2,1)S(1)}, u32[]{:S(2)}, u32[]{:S(2)}) %all-to-all-start.2) | async-done | bytes 655392 | tf_op jit(solution)/shard_map/all_to_all | solution.py:513
  194.8 0.0 copy-start.2
  194.8 0.8 copy-done.2
  195.6 1.9 unpack.1
  (17 shorter events, 0.3 us)
Async XLA Ops:
  0.6 20.4 %copy-start = (f32[50,7680]{1,0:T(8,128)S(1)}, f32[50,7680]{1,0:T(8,128)}, u32[]{:S(2)}) copy-start(f32[50,7680]{1,0:T(8,128)} %param.11) | copy-start | bytes 4608004
  5.6 11.9 %copy-start.8 = (f32[1,3,2560]{2,0,1:T(1,128)S(1)}, f32[1,3,2560]{2,0,1:T(1,128)}, u32[]{:S(2)}) copy-start(f32[1,3,2560]{2,0,1:T(1,128)} %param.14) | copy-start | bytes 92164
  5.6 11.9 %copy-start.6 = (f32[1,7680]{1,0:T(1,128)S(1)}, f32[1,7680]{1,0:T(1,128)}, u32[]{:S(2)}) copy-start(f32[1,7680]{1,0:T(1,128)} %param.13) | copy-start | bytes 92164
  5.6 11.9 %copy-start.7 = (f32[1,7680]{1,0:T(1,128)S(1)}, f32[1,7680]{1,0:T(1,128)}, u32[]{:S(2)}) copy-start(f32[1,7680]{1,0:T(1,128)} %param.12) | copy-start | bytes 92164
  5.6 15.5 %copy-start.9 = (s32[16]{0:T(128)S(1)}, s32[16]{0:T(128)}, u32[]{:S(2)}) copy-start(s32[16]{0:T(128)} %param.10) | copy-start | bytes 196
  5.6 78.2 %all-to-all-start = ((bf16[64,320,128]{2,1,0:T(8,128)(2,1)}), bf16[64,320,128]{2,1,0:T(8,128)(2,1)}, u32[]{:S(2)}, u32[]{:S(2)}) async-start(bf16[64,320,128]{2,1,0:T(8,128)(2,1)} %pack.1), calls=%async_computation | async-start | bytes 10485760 | tf_op jit(solution)/shard_map/all_to_all | solution.py:477
  17.5 18.0 %copy-start.4 = (f32[1,3,2560]{2,1,0:T(4,128)}, f32[1,3,2560]{2,1,0:T(4,128)S(1)}, u32[]{:S(2)}) copy-start(f32[1,3,2560]{2,1,0:T(4,128)S(1)} %copy.22) | copy-start | bytes 92164
  17.8 17.7 %collective-permute-start = (f32[6,2560]{1,0:T(8,128)S(1)}, f32[6,2560]{1,0:T(8,128)S(1)}, u32[]{:S(2)}, u32[]{:S(2)}) collective-permute-start(f32[6,2560]{1,0:T(8,128)S(1)} %pad_maximum_fusion.1), channel_id=1, source_target_pairs={{0,32},{32,0},{1,33},{33,1},{2,34},{34,2},{3,35},{35,3},{4,36},{36... | collective-permute-start | bytes 184328 | tf_op jit(solution)/shard_map/ppermute | solution.py:472
  104.7 13.4 %copy-start.3 = (bf16[1280,128]{1,0:T(8,128)(2,1)S(1)}, bf16[1280,128]{1,0:T(8,128)(2,1)}, u32[]{:S(2)}) copy-start(bf16[1280,128]{1,0:T(8,128)(2,1)} %get-tuple-element.4.x.own) | copy-start | bytes 983044
  106.9 36.1 %all-to-all-start.1 = ((bf16[64,64,128]{2,1,0:T(8,128)(2,1)}), bf16[64,64,128]{2,1,0:T(8,128)(2,1)S(1)}, u32[]{:S(2)}, u32[]{:S(2)}) async-start(bf16[64,64,128]{2,1,0:T(8,128)(2,1)} %middle.1), calls=%async_computation.1 | async-start | bytes 2097152 | tf_op jit(solution)/shard_map/all_to_all | solution.py:504
  118.2 19.6 %collective-permute-start.1 = (bf16[1280,128]{1,0:T(8,128)(2,1)S(1)}, bf16[1280,128]{1,0:T(8,128)(2,1)S(1)}, u32[]{:S(2)}, u32[]{:S(2)}) collective-permute-start(bf16[1280,128]{1,0:T(8,128)(2,1)S(1)} %copy-done.3), channel_id=1, source_target_pairs={{1,0},{2,1},{0,2},{5,4},{6,5},{4,6},{9,8},{10,9},{8,10},{13,12},{1... | collective-permute-start | bytes 983048 | tf_op jit(solution)/shard_map/ppermute | solution.py:500
  123.4 19.6 %collective-permute-start.2 = (bf16[1280,128]{1,0:T(8,128)(2,1)S(1)}, bf16[1280,128]{1,0:T(8,128)(2,1)}, u32[]{:S(2)}, u32[]{:S(2)}) collective-permute-start(bf16[1280,128]{1,0:T(8,128)(2,1)S(1)} %copy-done.3), channel_id=1, source_target_pairs={{2,0},{0,1},{1,2},{6,4},{4,5},{5,6},{10,8},{8,9},{9,10},{14,12},{1... | collective-permute-start | bytes 983048 | tf_op jit(solution)/shard_map/ppermute | solution.py:500
  137.8 5.2 %copy-start.5 = (bf16[1280,128]{1,0:T(8,128)(2,1)}, bf16[1280,128]{1,0:T(8,128)(2,1)S(1)}, u32[]{:S(2)}) copy-start(bf16[1280,128]{1,0:T(8,128)(2,1)S(1)} %collective-permute-done.1.after) | copy-start | bytes 983044
  142.9 1.0 copy-start.1
  164.5 1.8 collective-permute-start.3
  168.4 26.3 %all-to-all-start.2 = ((bf16[64,40,128]{2,1,0:T(8,128)(2,1)}), bf16[64,40,128]{2,1,0:T(8,128)(2,1)S(1)}, u32[]{:S(2)}, u32[]{:S(2)}) async-start(bf16[64,40,128]{2,1,0:T(8,128)(2,1)} %bitcast.12), calls=%async_computation.2 | async-start | bytes 1310720 | tf_op jit(solution)/shard_map/all_to_all | solution.py:513
  194.8 0.8 copy-start.2

commit v3 on v2

--- a/solution.py
+++ b/solution.py
@@ -149,114 +149,121 @@
     return jnp.concatenate([hot, aux, jnp.zeros((8, 128), F32)], axis=0).astype(BF16)
 
 
-def place_keys(p, kv, ka, vt):
-    row = lax.broadcasted_iota(jnp.int32, (128, 128), 0)
-    col = lax.broadcasted_iota(jnp.int32, (128, 128), 1)
-    at = pl.ds(pl.multiple_of(p * 128, 128), 128)
-    hidden = (col == p) | ((col == PATCHES) & (row >= TOK))
-    ka[at, 0:128] = kv[0, p, 0:128, :]
-    ka[at, 128:256] = jnp.where(hidden, -BIG, 0.0).astype(BF16)
-    vt[0:128, at] = kv[0, p, 128:256, :]
-    vt[128:144, at] = jnp.ones((16, 128), BF16)
-
-
-def place_pair(t, hids, maps, qa, of, mf):
+def modulations(kv, table, mods):
+    for begin in range(0, PATCHES, 8):
+        hot = [hot_rows(kv[0, p, 112:128, :].astype(F32)[8:16]) for p in range(begin, begin + 8)]
+        at = slice(begin * 128, begin * 128 + 1024)
+        mods[at, 0 : table.shape[1]] = dot(jnp.concatenate(hot, axis=1), table, TN)
+
+
+def place_pair(t, hids, maps, kv, qa, ka, vt, kf, vh):
     row = lax.broadcasted_iota(jnp.int32, (80, 128), 0)
     col = lax.broadcasted_iota(jnp.int32, (80, 128), 1)
     patch = 2 * t + jnp.where(row >= THIRD, 1, 0)
-    at = pl.ds(pl.multiple_of(t * 80, 16), 80)
-    q = (jnp.concatenate([hid[0:THIRD] for hid in hids], axis=0) * maps[0:1, :]).astype(BF16)
-    qa[at, 0:128] = q
+    at = slice(t * 80, t * 80 + 80)
+    q = jnp.concatenate([hid[0:THIRD] for hid in hids], axis=0) * maps[0:1, :]
+    qa[at, 0:128] = q.astype(BF16)
     qa[at, 128:256] = jnp.where((col == patch) | (col == PATCHES), 1.0, 0.0).astype(BF16)
-    keys = jnp.concatenate([(hid * maps[1:2, :]).astype(BF16) for hid in hids], axis=0)
-    vals = jnp.concatenate([(hid * maps[2:3, :]).astype(BF16) for hid in hids], axis=0)
-    s = dot(q, keys, NT)
-    s = jnp.concatenate([s[0:THIRD, 0:128], s[THIRD:80, 128:256]], axis=0)
-    s = jnp.where(col < TOK, s, -BIG)
-    top = jnp.max(s, axis=1, keepdims=True)
-    power = jnp.exp2((s - top) * FACTOR)
-    none = jnp.zeros((THIRD, 128), F32)
-    both = [
-        jnp.concatenate([power[0:THIRD], none], axis=1),
-        jnp.concatenate([none, power[THIRD:80]], axis=1),
-    ]
-    both = jnp.concatenate(both, axis=0).astype(BF16)
-    vals = jnp.concatenate([vals, jnp.ones((256, 128), BF16)], axis=1)
-    of[at, :] = dot(both, vals, NN)
-    mf[at, :] = jnp.broadcast_to(top, (80, 128))
-
-
-def attention(qa, ka, vt, of, mf, xo, go, sc, pt, result):
+    row = lax.broadcasted_iota(jnp.int32, (128, 128), 0)
+    col = lax.broadcasted_iota(jnp.int32, (128, 128), 1)
+    for half in range(2):
+        p = 2 * t + half
+        at = slice(p * 128, p * 128 + 128)
+        ka[at, 0:128] = kv[0, p, 0:128, :]
+        hidden = (col == p) | ((col == PATCHES) & (row >= TOK))
+        ka[at, 128:256] = jnp.where(hidden, -BIG, 0.0).astype(BF16)
+        vt[0:128, at] = kv[0, p, 128:256, :]
+        kf[at, 0:128] = (hids[half] * maps[1:2, :]).astype(BF16)
+        hidden = (col <= PATCHES) & ((row >= TOK) | ((col != p) & (col < PATCHES)))
+        kf[at, 128:256] = jnp.where(hidden, -BIG, 0.0).astype(BF16)
+        vh[at, :] = (hids[half] * maps[2:3, :]).astype(BF16)
+
+
+def turn_values(vh, vt, vf):
+    row = lax.broadcasted_iota(jnp.int32, (128, 128), 0)
+    col = lax.broadcasted_iota(jnp.int32, (128, 128), 1)
+    unit = jnp.where(row == col, 1.0, 0.0).astype(BF16)
+    for begin in range(0, PATCHES * 128, 1024):
+        at = slice(begin, begin + 1024)
+        vf[0:128, at] = dot(unit, vh[at, :], NT).astype(BF16)
+    vt[128:144, :] = jnp.ones((16, PATCHES * 128), BF16)
+    vf[128:144, :] = jnp.ones((16, PATCHES * 128), BF16)
+
+
+def attention(qa, ka, vt, kf, vf, xo, go, sc, pt, result):
     step = 512
-    begins = range(0, PATCHES * 128, step)
-    tiles = OWN_ROWS // TILE
-    tops = [None] * tiles
-
-    def score(tile, begin):
-        s = dot(ka[begin : begin + step, :], qa[tile * TILE : tile * TILE + TILE, :], NT)
-        sc[tile % 2, begin : begin + step, :] = s
-        top = jnp.max(s.reshape(step // 8, 8, TILE), axis=0)
-        tops[tile] = top if begin == 0 else jnp.maximum(tops[tile], top)
-
-    def weigh(tile, begin, top):
-        s = sc[tile % 2, begin : begin + step, :]
-        pt[tile % 2, begin : begin + step, :] = jnp.exp2((s - top) * FACTOR).astype(BF16)
-
-    def finish(tile, top):
-        total = dot(vt[...], pt[tile % 2], NN)
-        own = total[0:128].T
-        stats = jnp.concatenate([total[128:136], jnp.broadcast_to(top, (8, TILE))], axis=0).T
-        at = slice(tile * TILE, tile * TILE + TILE)
-        top_s, top_f = stats[:, 8:9], mf[at, 0:1]
-        top = jnp.maximum(top_s, top_f)
-        a, b = jnp.exp2((top_s - top) * FACTOR), jnp.exp2((top_f - top) * FACTOR)
-        fresh = of[at, :]
-        attended = (a * own + b * fresh[:, 0:128]) / (a * stats[:, 0:1] + b * fresh[:, 128:256])
-        result(at, (xo[at, :] + go[at, :] * attended).astype(BF16))
-
-    for begin in begins:
-        score(0, begin)
-    for tile in range(tiles):
-        top = jnp.max(tops[tile], axis=0, keepdims=True)
+    stale = PATCHES * 128
+    begins = range(0, stale + step, step)
+    row = lax.broadcasted_iota(jnp.int32, (128, 256), 0)
+    col = lax.broadcasted_iota(jnp.int32, (128, 256), 1)
+    unit = jnp.where((row == col) | (row + 128 == col), 1.0, 0.0).astype(BF16)
+
+    def fresh_at(tile, j):
+        low = (tile * (TILE // THIRD) + 3 * j) * 128
+        return slice(low, low + step)
+
+    for tile in range(OWN_ROWS // TILE):
+        first = tile * TILE
+        top = None
         for begin in begins:
-            if tile + 1 < tiles:
-                score(tile + 1, begin)
-            weigh(tile, begin, top)
-        finish(tile, top)
-
-
-def first_kernel(kv, x_rest, frame_mod, maps, x_out, sums, qa, ka, vt, of, mf, xo, go, sc, pt, sq):
+            if begin < stale:
+                s = dot(ka[begin : begin + step, :], qa[first : first + TILE, :], NT)
+            else:
+                parts = [
+                    dot(kf[fresh_at(tile, j), :], qa[first + 128 * j : first + 128 * j + 128, :], NT)
+                    for j in range(TILE // 128)
+                ]
+                s = jnp.concatenate(parts, axis=1)
+            sc[begin : begin + step, :] = s
+            here = jnp.max(s.reshape(step // 8, 8, TILE), axis=0)
+            top = here if top is None else jnp.maximum(top, here)
+        top = jnp.max(top, axis=0, keepdims=True)
+        for begin in begins:
+            pt[begin : begin + step, :] = jnp.exp2((sc[begin : begin + step, :] - top) * FACTOR).astype(BF16)
+        total = dot(vt[...], pt[0:stale, :], NN)
+        more = [
+            dot(vf[:, fresh_at(tile, j)], pt[stale : stale + step, 128 * j : 128 * j + 128], NN)
+            for j in range(TILE // 128)
+        ]
+        total = total + jnp.concatenate(more, axis=1)
+        mean = total[0:128] / total[128:129]
+        hi = mean.astype(BF16)
+        low = (mean - hi.astype(F32)).astype(BF16)
+        for j in range(TILE // 128):
+            cols = slice(128 * j, 128 * j + 128)
+            attended = dot(unit, jnp.concatenate([hi[:, cols], low[:, cols]], axis=1), NT)
+            at = slice(first + 128 * j, first + 128 * j + 128)
+            result(at, (xo[at, :] + go[at, :] * attended).astype(BF16))
+
+
+def first_kernel(kv, x_rest, frame_mod, maps, x_out, sums, qa, ka, vt, kf, vf, xo, go, sc, pt, mods, vh, sq):
     table = mod_table(frame_mod[...], True)
     gains = maps[...]
 
-    @pl.loop(0, 4)
-    def _(block):
-        for sub in range(4):
-            t = block * 4 + sub
-            hids, xs, gates = [], [], []
-            for half in range(2):
-                p = 2 * t + half
-                aux = kv[0, p, 112:128, :].astype(F32)[8:16]
-                xa = kv[0, p, 256:CHUNK, :].astype(F32)
-                xb = x_rest[0, p].astype(F32)[8:64]
-                x = jnp.concatenate([xa, xb, jnp.zeros((8, 128), F32)], axis=0)
-                m = dot(hot_rows(aux), table, TN)
-                hid = x * m[:, 384:512] * (1.0 + m[:, 128:256]) + m[:, 0:128]
-                place_keys(p, kv, ka, vt)
-                hids.append(hid)
-                xs.append(x[0:THIRD])
-                gates.append(m[0:THIRD, 256:384])
-            place_pair(t, hids, gains, qa, of, mf)
-            at = pl.ds(pl.multiple_of(t * 80, 16), 80)
-            xo[at, :] = jnp.concatenate(xs, axis=0)
-            go[at, :] = jnp.concatenate(gates, axis=0)
+    modulations(kv, table, mods)
+    for t in range(PATCHES // 2):
+        at = slice(t * 80, t * 80 + 80)
+        hids, xs, gates = [], [], []
+        for half in range(2):
+            p = 2 * t + half
+            xa = kv[0, p, 256:CHUNK, :].astype(F32)
+            xb = x_rest[0, p].astype(F32)[8:64]
+            x = jnp.concatenate([xa, xb, jnp.zeros((8, 128), F32)], axis=0)
+            m = mods[p * 128 : p * 128 + 128, :]
+            hids.append(x * m[:, 384:512] * (1.0 + m[:, 128:256]) + m[:, 0:128])
+            xs.append(x[0:THIRD])
+            gates.append(m[0:THIRD, 256:384])
+        place_pair(t, hids, gains, kv, qa, ka, vt, kf, vh)
+        xo[at, :] = jnp.concatenate(xs, axis=0)
+        go[at, :] = jnp.concatenate(gates, axis=0)
+    turn_values(vh, vt, vf)
 
     def result(at, value):
         x_out[at, :] = value
         wide = value.astype(F32)
         sq[at, :] = wide * wide
 
-    attention(qa, ka, vt, of, mf, xo, go, sc, pt, result)
+    attention(qa, ka, vt, kf, vf, xo, go, sc, pt, result)
     square = sq[...]
     hi = square.astype(BF16)
     low = (square - hi.astype(F32)).astype(BF16)
@@ -295,12 +302,14 @@
     pltpu.VMEM((OWN_ROWS, 256), BF16),
     pltpu.VMEM((PATCHES * 128, 256), BF16),
     pltpu.VMEM((144, PATCHES * 128), BF16),
-    pltpu.VMEM((OWN_ROWS, 256), F32),
+    pltpu.VMEM((PATCHES * 128, 256), BF16),
+    pltpu.VMEM((144, PATCHES * 128), BF16),
     pltpu.VMEM((OWN_ROWS, 128), F32),
     pltpu.VMEM((OWN_ROWS, 128), F32),
-    pltpu.VMEM((OWN_ROWS, 128), F32),
-    pltpu.VMEM((2, PATCHES * 128, TILE), F32),
-    pltpu.VMEM((2, PATCHES * 128, TILE), BF16),
+    pltpu.VMEM((PATCHES * 128 + 512, TILE), F32),
+    pltpu.VMEM((PATCHES * 128 + 512, TILE), BF16),
+    pltpu.VMEM((PATCHES * 128, 512), F32),
+    pltpu.VMEM((PATCHES * 128, 128), BF16),
 ]
 
 
@@ -328,7 +337,7 @@
     )(received, received, frame_mod, maps)
 
 
-def second_kernel(scal, kv, own, after, before, sums, frame_mod, maps, x_out, qa, ka, vt, of, mf, xo, go, sc, pt, rs):
+def second_kernel(scal, kv, own, after, before, sums, frame_mod, maps, x_out, qa, ka, vt, kf, vf, xo, go, sc, pt, mods, vh, rs):
     table = mod_table(frame_mod[...], False)
     gains = maps[...]
     third = scal[0]
@@ -346,34 +355,30 @@
         r = jnp.where(row == 0, hi, jnp.where(row == 1, mid, jnp.where(row == 2, low, 0.0)))
         rs[k] = dot(r.astype(BF16), ones, TN)
 
-    @pl.loop(0, 4)
-    def _(block):
-        for sub in range(4):
-            t = block * 4 + sub
-            at = pl.ds(pl.multiple_of(t * 80, 16), 80)
-            pair = [ref[at, :].astype(F32) for ref in (own, after, before)]
-            scale = [rs[k, at, :] for k in range(3)]
-            hids, gates = [], []
-            for half in range(2):
-                p = 2 * t + half
-                cut = slice(THIRD * half, THIRD * half + THIRD)
-                aux = kv[0, p, 112:128, :].astype(F32)[8:16]
-                none = [jnp.zeros((8, 128), F32)]
-                x = jnp.concatenate([v[cut] for v in pair] + none, axis=0)
-                r = jnp.concatenate([v[cut] for v in scale] + none, axis=0)
-                m = dot(hot_rows(aux), table, TN)
-                hid = x * r * (1.0 + m[:, 128:256]) + m[:, 0:128]
-                place_keys(p, kv, ka, vt)
-                hids.append(hid)
-                gates.append(m[0:THIRD, 256:384])
-            place_pair(t, hids, gains, qa, of, mf)
-            xo[at, :] = pair[0]
-            go[at, :] = jnp.concatenate(gates, axis=0)
+    modulations(kv, table, mods)
+    for t in range(PATCHES // 2):
+        at = slice(t * 80, t * 80 + 80)
+        pair = [ref[at, :].astype(F32) for ref in (own, after, before)]
+        scale = [rs[k, at, :] for k in range(3)]
+        hids, gates = [], []
+        for half in range(2):
+            p = 2 * t + half
+            cut = slice(THIRD * half, THIRD * half + THIRD)
+            none = [jnp.zeros((8, 128), F32)]
+            x = jnp.concatenate([v[cut] for v in pair] + none, axis=0)
+            r = jnp.concatenate([v[cut] for v in scale] + none, axis=0)
+            m = mods[p * 128 : p * 128 + 128, 0:384]
+            hids.append(x * r * (1.0 + m[:, 128:256]) + m[:, 0:128])
+            gates.append(m[0:THIRD, 256:384])
+        place_pair(t, hids, gains, kv, qa, ka, vt, kf, vh)
+        xo[at, :] = pair[0]
+        go[at, :] = jnp.concatenate(gates, axis=0)
+    turn_values(vh, vt, vf)
 
     def result(at, value):
         x_out[at, :] = value
 
-    attention(qa, ka, vt, of, mf, xo, go, sc, pt, result)
+    attention(qa, ka, vt, kf, vf, xo, go, sc, pt, result)
 
 
 def second_layer(third, received, own, after, before, sums, frame_mod, maps):

time: 198 us -> 188 us (0.949)
  Pallas kernels: 53.7 us -> 43.6 us
    pallas_call x1, Pallas kernels: 20.9 us -> 15.6 us  [first_layer(): pl.pallas_call(first_kernel, grid=(1,), in_specs=[pl.BlockSpec((1, PATCHE...]
    pallas_call x1, Pallas kernels: 20.6 us -> 15.8 us  [second_layer(): pl.pallas_call(second_kernel, grid_spec=grid, out_shape=jax.ShapeDtypeStr...]
where the time goes in v3:
time: 188 us; the launch traced here: 187 us
  waiting for transfers between devices  90.5 us (48%)
  starting transfers between devices  44.5 us (24%)
  Pallas kernels  43.6 us (23%)
  local copies, waits for them, and re-layouts  4.88 us (3%)
    all_to_all x1, waiting for transfers between devices, body(): received = lax.all_to_all(send, PLANE, 0, 0, tiled=True)  46.9 us
    ppermute x2, waiting for transfers between devices, from_third(): return lax.ppermute(x_one, PLANE, pairs)  17.2 us
    pallas_call x1, Pallas kernels, second_layer(): pl.pallas_call(second_kernel, grid_spec=grid, out_shape=jax.ShapeDtypeStr...  15.8 us
    pallas_call x1, Pallas kernels, first_layer(): pl.pallas_call(first_kernel, grid=(1,), in_specs=[pl.BlockSpec((1, PATCHE...  15.6 us
    ppermute x1, waiting for transfers between devices, body(): other = lax.ppermute(both, 'section', [(0, 1), (1, 0)])  12.8 us
    all_to_all x1, starting transfers between devices, body(): received = lax.all_to_all(send, PLANE, 0, 0, tiled=True)  11.9 us
    all_to_all x1, waiting for transfers between devices, body(): guided_got = lax.all_to_all(guided, PLANE, 0, 0, tiled=True)  11.8 us
    all_to_all x1, starting transfers between devices, body(): guided_got = lax.all_to_all(guided, PLANE, 0, 0, tiled=True)  11.3 us
  transfers between devices with their start and end apart: 7, of which 6 were waited for; matrix products, arithmetic and copies ran while one was open for 2% of the time, Pallas kernels for 2%

profile of v3, /device:TPU:0, one launch (start us, length us, event | category | flops | bytes accessed | tf_op | source)
XLA Modules:
  0.0 187.4 jit_solution(9754514938419551606)
XLA Ops:
  0.6 0.0 copy-start
  0.7 4.9 %pack.1 = bf16[64,320,128]{2,1,0:T(8,128)(2,1)} custom-call(s32[1]{0:T(128)} %bitcast.2.scal, bf16[2,120,2560]{2,1,0:T(8,128)(2,1)} %bitcast.39, bf16[120,2560]{1,0:T(8,128)(2,1)} %stream.3, s32[1,120]{1,0:T(1,128)} %bitcast.49), custom_call_target="tpu_custom_call" | custom-call | tf_op jit(solution)/shard_map/pack/pallas_call | solution.py:127
  5.6 0.0 copy-start.8
  5.6 0.0 copy-start.6
  5.6 0.0 copy-start.7
  5.6 0.0 copy-start.9
  5.6 11.9 %all-to-all-start = ((bf16[64,320,128]{2,1,0:T(8,128)(2,1)}), bf16[64,320,128]{2,1,0:T(8,128)(2,1)}, u32[]{:S(2)}, u32[]{:S(2)}) async-start(bf16[64,320,128]{2,1,0:T(8,128)(2,1)} %pack.1), calls=%async_computation | async-start | bytes 10485760 | tf_op jit(solution)/shard_map/all_to_all | solution.py:482
  17.5 0.0 copy-done.8
  17.5 0.0 copy-done.6
  17.5 0.0 copy-done.7
  17.5 0.0 copy-start.4
  17.6 0.2 add_reduce_fusion
  17.8 3.2 %collective-permute-start = (f32[6,2560]{1,0:T(8,128)S(1)}, f32[6,2560]{1,0:T(8,128)S(1)}, u32[]{:S(2)}, u32[]{:S(2)}) collective-permute-start(f32[6,2560]{1,0:T(8,128)S(1)} %pad_maximum_fusion.1), channel_id=1, source_target_pairs={{0,32},{32,0},{1,33},{33,1},{2,34},{34,2},{3,35},{35,3},{4,36},{36... | collective-permute-start | bytes 184328 | tf_op jit(solution)/shard_map/ppermute | solution.py:477
  21.1 0.0 copy-done
  21.1 0.0 copy-done.9
  21.1 1.5 broadcast_add_fusion
  22.6 0.1 reshape.47
  22.7 12.8 %collective-permute-done = f32[6,2560]{1,0:T(8,128)S(1)} collective-permute-done((f32[6,2560]{1,0:T(8,128)S(1)}, f32[6,2560]{1,0:T(8,128)S(1)}, u32[]{:S(2)}, u32[]{:S(2)}) %collective-permute-start) | collective-permute-done | bytes 61472 | tf_op jit(solution)/shard_map/ppermute | solution.py:477
  35.5 0.0 copy-done.4
  35.7 0.6 copy.24
  36.3 0.6 slice_bitcast_fusion
  36.9 46.9 %all-to-all-done = bf16[64,320,128]{2,1,0:T(8,128)(2,1)} async-done(((bf16[64,320,128]{2,1,0:T(8,128)(2,1)}), bf16[64,320,128]{2,1,0:T(8,128)(2,1)}, u32[]{:S(2)}, u32[]{:S(2)}) %all-to-all-start) | async-done | bytes 5242912 | tf_op jit(solution)/shard_map/all_to_all | solution.py:482
  83.8 15.6 %first_layer.1 = (bf16[1280,128]{1,0:T(8,128)(2,1)}, f32[8,1280]{1,0:T(8,128)}) custom-call(bf16[2,32,320,128]{3,2,1,0:T(8,128)(2,1)} %bitcast.5.kv.x_rest, bf16[2,32,320,128]{3,2,1,0:T(8,128)(2,1)} %bitcast.5.kv.x_rest, f32[16,384]{1,0:T(8,128)} %bitcast.46, f32[3,128]{1,0:T(4,128)} %get-tuple-element.14.maps), custom_call_target="tpu_custom_call" | custom-call | tf_op jit(solution)/shard_map/first_layer/pallas_call | solution.py:317
  99.4 0.0 copy-start.3
  99.4 2.1 %middle.1 = bf16[64,64,128]{2,1,0:T(8,128)(2,1)} custom-call(bf16[1280,128]{1,0:T(8,128)(2,1)} %get-tuple-element.4.x.own, f32[8,1280]{1,0:T(8,128)} %get-tuple-element.5.total), custom_call_target="tpu_custom_call" | custom-call | tf_op jit(solution)/shard_map/middle/pallas_call | solution.py:291
  101.5 11.3 %all-to-all-start.1 = ((bf16[64,64,128]{2,1,0:T(8,128)(2,1)}), bf16[64,64,128]{2,1,0:T(8,128)(2,1)S(1)}, u32[]{:S(2)}, u32[]{:S(2)}) async-start(bf16[64,64,128]{2,1,0:T(8,128)(2,1)} %middle.1), calls=%async_computation.1 | async-start | bytes 2097152 | tf_op jit(solution)/shard_map/all_to_all | solution.py:509
  112.8 0.0 copy-done.3
  112.8 5.0 %collective-permute-start.1 = (bf16[1280,128]{1,0:T(8,128)(2,1)S(1)}, bf16[1280,128]{1,0:T(8,128)(2,1)S(1)}, u32[]{:S(2)}, u32[]{:S(2)}) collective-permute-start(bf16[1280,128]{1,0:T(8,128)(2,1)S(1)} %copy-done.3), channel_id=1, source_target_pairs={{1,0},{2,1},{0,2},{5,4},{6,5},{4,6},{9,8},{10,9},{8,10},{13,12},{1... | collective-permute-start | bytes 983048 | tf_op jit(solution)/shard_map/ppermute | solution.py:505
  117.8 1.9 %collective-permute-start.2 = (bf16[1280,128]{1,0:T(8,128)(2,1)S(1)}, bf16[1280,128]{1,0:T(8,128)(2,1)}, u32[]{:S(2)}, u32[]{:S(2)}) collective-permute-start(bf16[1280,128]{1,0:T(8,128)(2,1)S(1)} %copy-done.3), channel_id=1, source_target_pairs={{2,0},{0,1},{1,2},{6,4},{4,5},{5,6},{10,8},{8,9},{9,10},{14,12},{1... | collective-permute-start | bytes 983048 | tf_op jit(solution)/shard_map/ppermute | solution.py:505
  119.8 0.6 copy.23
  120.4 12.1 %collective-permute-done.1.after = bf16[1280,128]{1,0:T(8,128)(2,1)S(1)} collective-permute-done((bf16[1280,128]{1,0:T(8,128)(2,1)S(1)}, bf16[1280,128]{1,0:T(8,128)(2,1)S(1)}, u32[]{:S(2)}, u32[]{:S(2)}) %collective-permute-start.1) | collective-permute-done | bytes 327712 | tf_op jit(solution)/shard_map/ppermute | solution.py:505
  132.4 0.0 copy-start.5
  132.4 5.2 %collective-permute-done.2.before = bf16[1280,128]{1,0:T(8,128)(2,1)} collective-permute-done((bf16[1280,128]{1,0:T(8,128)(2,1)S(1)}, bf16[1280,128]{1,0:T(8,128)(2,1)}, u32[]{:S(2)}, u32[]{:S(2)}) %collective-permute-start.2) | collective-permute-done | bytes 327712 | tf_op jit(solution)/shard_map/ppermute | solution.py:505
  137.6 0.0 all-to-all-done.1.sums.got
  137.6 0.0 copy-start.1
  137.6 0.0 copy-done.5
  137.6 1.0 copy-done.1
  138.6 15.8 %second_layer.1 = bf16[1280,128]{1,0:T(8,128)(2,1)} custom-call(s32[1]{0:T(128)} %bitcast.1.scal, bf16[2,32,320,128]{3,2,1,0:T(8,128)(2,1)} %bitcast.5.kv.x_rest, bf16[1280,128]{1,0:T(8,128)(2,1)} %get-tuple-element.4.x.own, bf16[1280,128]{1,0:T(8,128)(2,1)} %copy-done.5, bf16[1280,128]{1,0:T(8,128)(2,1)} %collective-permute-done.2.before, ...), custom_call_target="tpu_custom_call" | custom-call | tf_op jit(solution)/shard_map/second_layer/pallas_call | solution.py:401
  154.4 0.0 collective-permute-start.3
  154.4 1.8 collective-permute-done.3
  156.2 1.1 fusion.1
  157.3 0.9 broadcast_in_dim.7
  158.3 11.3 %all-to-all-start.2 = ((bf16[64,40,128]{2,1,0:T(8,128)(2,1)}), bf16[64,40,128]{2,1,0:T(8,128)(2,1)S(1)}, u32[]{:S(2)}, u32[]{:S(2)}) async-start(bf16[64,40,128]{2,1,0:T(8,128)(2,1)} %bitcast.12), calls=%async_computation.2 | async-start | bytes 1310720 | tf_op jit(solution)/shard_map/all_to_all | solution.py:518
  169.6 3.3 %home.1 = bf16[2,120,2560]{2,1,0:T(8,128)(2,1)} custom-call(s32[1]{0:T(128)} %bitcast.2.scal, bf16[64,64,128]{2,1,0:T(8,128)(2,1)} %copy-done.1, bf16[120,2560]{1,0:T(8,128)(2,1)} %stream.3, s32[1,120]{1,0:T(1,128)} %bitcast.50, f32[16,7680]{1,0:T(8,128)} %get-tuple-element.15.frame_mod, f32[3,2560]{1,0:T(4,128)} %bitcast.42), custom_call_target="tpu_custom_call" | custom-call | tf_op jit(solution)/shard_map/home/pallas_call | solution.py:435
  172.9 11.8 %all-to-all-done.2.got = bf16[64,40,128]{2,1,0:T(8,128)(2,1)S(1)} async-done(((bf16[64,40,128]{2,1,0:T(8,128)(2,1)}), bf16[64,40,128]{2,1,0:T(8,128)(2,1)S(1)}, u32[]{:S(2)}, u32[]{:S(2)}) %all-to-all-start.2) | async-done | bytes 655392 | tf_op jit(solution)/shard_map/all_to_all | solution.py:518
  184.6 0.0 copy-start.2
  184.6 0.8 copy-done.2
  185.5 1.9 %unpack.1 = bf16[120,1280]{1,0:T(8,128)(2,1)} custom-call(s32[1]{0:T(128)} %bitcast.scal, bf16[64,40,128]{2,1,0:T(8,128)(2,1)} %copy-done.2), custom_call_target="tpu_custom_call" | custom-call | tf_op jit(solution)/shard_map/unpack/pallas_call | solution.py:458
  (17 shorter events, 0.3 us)
Async XLA Ops:
  0.6 20.4 %copy-start = (f32[50,7680]{1,0:T(8,128)S(1)}, f32[50,7680]{1,0:T(8,128)}, u32[]{:S(2)}) copy-start(f32[50,7680]{1,0:T(8,128)} %param.11) | copy-start | bytes 4608004
  5.6 11.9 %copy-start.8 = (f32[1,3,2560]{2,0,1:T(1,128)S(1)}, f32[1,3,2560]{2,0,1:T(1,128)}, u32[]{:S(2)}) copy-start(f32[1,3,2560]{2,0,1:T(1,128)} %param.14) | copy-start | bytes 92164
  5.6 11.9 %copy-start.6 = (f32[1,7680]{1,0:T(1,128)S(1)}, f32[1,7680]{1,0:T(1,128)}, u32[]{:S(2)}) copy-start(f32[1,7680]{1,0:T(1,128)} %param.13) | copy-start | bytes 92164
  5.6 11.9 %copy-start.7 = (f32[1,7680]{1,0:T(1,128)S(1)}, f32[1,7680]{1,0:T(1,128)}, u32[]{:S(2)}) copy-start(f32[1,7680]{1,0:T(1,128)} %param.12) | copy-start | bytes 92164
  5.6 15.5 %copy-start.9 = (s32[16]{0:T(128)S(1)}, s32[16]{0:T(128)}, u32[]{:S(2)}) copy-start(s32[16]{0:T(128)} %param.10) | copy-start | bytes 196
  5.6 78.2 %all-to-all-start = ((bf16[64,320,128]{2,1,0:T(8,128)(2,1)}), bf16[64,320,128]{2,1,0:T(8,128)(2,1)}, u32[]{:S(2)}, u32[]{:S(2)}) async-start(bf16[64,320,128]{2,1,0:T(8,128)(2,1)} %pack.1), calls=%async_computation | async-start | bytes 10485760 | tf_op jit(solution)/shard_map/all_to_all | solution.py:482
  17.5 18.0 %copy-start.4 = (f32[1,3,2560]{2,1,0:T(4,128)}, f32[1,3,2560]{2,1,0:T(4,128)S(1)}, u32[]{:S(2)}) copy-start(f32[1,3,2560]{2,1,0:T(4,128)S(1)} %copy.22) | copy-start | bytes 92164
  17.8 17.7 %collective-permute-start = (f32[6,2560]{1,0:T(8,128)S(1)}, f32[6,2560]{1,0:T(8,128)S(1)}, u32[]{:S(2)}, u32[]{:S(2)}) collective-permute-start(f32[6,2560]{1,0:T(8,128)S(1)} %pad_maximum_fusion.1), channel_id=1, source_target_pairs={{0,32},{32,0},{1,33},{33,1},{2,34},{34,2},{3,35},{35,3},{4,36},{36... | collective-permute-start | bytes 184328 | tf_op jit(solution)/shard_map/ppermute | solution.py:477
  99.4 13.4 %copy-start.3 = (bf16[1280,128]{1,0:T(8,128)(2,1)S(1)}, bf16[1280,128]{1,0:T(8,128)(2,1)}, u32[]{:S(2)}) copy-start(bf16[1280,128]{1,0:T(8,128)(2,1)} %get-tuple-element.4.x.own) | copy-start | bytes 983044
  101.5 36.1 %all-to-all-start.1 = ((bf16[64,64,128]{2,1,0:T(8,128)(2,1)}), bf16[64,64,128]{2,1,0:T(8,128)(2,1)S(1)}, u32[]{:S(2)}, u32[]{:S(2)}) async-start(bf16[64,64,128]{2,1,0:T(8,128)(2,1)} %middle.1), calls=%async_computation.1 | async-start | bytes 2097152 | tf_op jit(solution)/shard_map/all_to_all | solution.py:509
  112.8 19.6 %collective-permute-start.1 = (bf16[1280,128]{1,0:T(8,128)(2,1)S(1)}, bf16[1280,128]{1,0:T(8,128)(2,1)S(1)}, u32[]{:S(2)}, u32[]{:S(2)}) collective-permute-start(bf16[1280,128]{1,0:T(8,128)(2,1)S(1)} %copy-done.3), channel_id=1, source_target_pairs={{1,0},{2,1},{0,2},{5,4},{6,5},{4,6},{9,8},{10,9},{8,10},{13,12},{1... | collective-permute-start | bytes 983048 | tf_op jit(solution)/shard_map/ppermute | solution.py:505
  117.8 19.8 %collective-permute-start.2 = (bf16[1280,128]{1,0:T(8,128)(2,1)S(1)}, bf16[1280,128]{1,0:T(8,128)(2,1)}, u32[]{:S(2)}, u32[]{:S(2)}) collective-permute-start(bf16[1280,128]{1,0:T(8,128)(2,1)S(1)} %copy-done.3), channel_id=1, source_target_pairs={{2,0},{0,1},{1,2},{6,4},{4,5},{5,6},{10,8},{8,9},{9,10},{14,12},{1... | collective-permute-start | bytes 983048 | tf_op jit(solution)/shard_map/ppermute | solution.py:505
  132.4 5.2 %copy-start.5 = (bf16[1280,128]{1,0:T(8,128)(2,1)}, bf16[1280,128]{1,0:T(8,128)(2,1)S(1)}, u32[]{:S(2)}) copy-start(bf16[1280,128]{1,0:T(8,128)(2,1)S(1)} %collective-permute-done.1.after) | copy-start | bytes 983044
  137.6 1.0 copy-start.1
  154.4 1.8 collective-permute-start.3
  158.3 26.4 %all-to-all-start.2 = ((bf16[64,40,128]{2,1,0:T(8,128)(2,1)}), bf16[64,40,128]{2,1,0:T(8,128)(2,1)S(1)}, u32[]{:S(2)}, u32[]{:S(2)}) async-start(bf16[64,40,128]{2,1,0:T(8,128)(2,1)} %bitcast.12), calls=%async_computation.2 | async-start | bytes 1310720 | tf_op jit(solution)/shard_map/all_to_all | solution.py:518
  184.6 0.8 copy-start.2
